TPU v7x, 128 devices: a whole 4x4x4 slice. The times are simulated.
128 devices in a mesh: ep: 8 (over z, core), etp: 4 (over y), dp: 4 (over x).
Axes of the slice: x: 4, y: 4, z: 4, core: 2. Of those that a mesh axis runs over, the one named last changes fastest.
Arguments:
- inputs: bfloat16 [32768, 4096], P(('ep', 'etp', 'dp')), may hold values from -6 to 6
- upstream: bfloat16 [32768, 4096], P(('ep', 'etp', 'dp')), may hold values from -24 to 24
- experts: int32 [32768, 8], P(('ep', 'etp', 'dp')), may hold values from 0 to 127, all different within a row
- gate_probs: float32 [32768, 8], P(('ep', 'etp', 'dp')), may hold values from 0.05 to 0.5
- gate_weight: bfloat16 [8, 4096, 1536], P('ep', None, 'etp'), may hold values from -0.09375 to 0.09375
- up_weight: bfloat16 [8, 4096, 1536], P('ep', None, 'etp'), may hold values from -0.09375 to 0.09375
- down_weight: bfloat16 [8, 1536, 4096], P('ep', 'etp'), may hold values from -0.15625 to 0.15625
Outputs:
- grad_inputs: bfloat16 [32768, 4096], P(('ep', 'etp', 'dp'))
- grad_probs: float32 [32768, 8], P(('ep', 'etp', 'dp'))
- grad_gate: bfloat16 [8, 4096, 1536], P('ep', 'dp', 'etp')
- grad_up: bfloat16 [8, 4096, 1536], P('ep', 'dp', 'etp')
- grad_down: bfloat16 [8, 1536, 4096], P('ep', 'etp', 'dp')
All inputs are finite; a program needn't handle non-finite values.
Results may differ from a plain program's by a relative error of at most 0.013.
Values may be sent and summed in bfloat16 or wider, within the bound.
No kernel may reach another device: no remote copies, remote signals or barrier semaphores. Data moves between devices by JAX's collectives and lax.ppermute only.
A program may use at most 128 MiB of HBM per device.

v0:
```python
import functools

import jax
import jax.numpy as jnp
from jax import lax
from jax.experimental import pallas as pl
from jax.experimental.pallas import tpu as pltpu
from jax.sharding import PartitionSpec as P

CAP = 24
LANES = 128
F32 = jnp.float32
BF = jnp.bfloat16
MIB = 2**20
BY_LAST = (((1,), (1,)), ((), ()))
BY_FIRST = (((0,), (0,)), ((), ()))


def dot(a, b):
    return jnp.dot(a, b, preferred_element_type=F32)


def cost(flops, size):
    return pl.CostEstimate(flops=int(flops), bytes_accessed=int(size), transcendentals=0)


def limit(mib):
    return pltpu.CompilerParams(vmem_limit_bytes=mib * MIB)


def slot_tables(expert_rows, prob_rows, expert_ids, capacity):
    tok_rows = expert_rows.shape[0]
    chosen = expert_rows[:, :, None] == expert_ids[None, None, :]
    member = jnp.any(chosen, axis=1)
    weight = jnp.sum(jnp.where(chosen, prob_rows[:, :, None], 0.0), axis=1)
    order_in = jnp.cumsum(member.astype(jnp.int32), axis=0) - 1
    slot_ids = jnp.arange(capacity, dtype=jnp.int32)
    onehot = member.T[:, None, :] & (order_in.T[:, None, :] == slot_ids[None, :, None])
    slot_gate = jnp.sum(jnp.where(onehot, weight.T[:, None, :], 0.0), axis=2)
    return onehot, chosen, slot_gate


def pick_kernel(onehot_ref, gate_ref, x_ref, dy_ref, own_ref, other_ref):
    step = pl.program_id(0)
    half = pl.num_programs(0) // 2
    mid = own_ref.shape[0]

    @pl.when(step < half)
    def _():
        rows = dot(onehot_ref[...], x_ref[...]).astype(BF)
        own_ref[...] = rows[:mid]
        other_ref[...] = rows[mid:]

    @pl.when(step >= half)
    def _():
        rows = (dot(onehot_ref[...], dy_ref[...]) * gate_ref[...]).astype(BF)
        own_ref[...] = rows[:mid]
        other_ref[...] = rows[mid:]


def pick_rows(onehot, gate, inputs, upstream):
    slots, tokens = onehot.shape
    width = inputs.shape[1]
    block = 1024
    half = width // block
    out = jax.ShapeDtypeStruct((slots // 2, 2 * width), BF)
    spec = pl.BlockSpec((slots // 2, block), lambda i: (0, i))
    return pl.pallas_call(
        pick_kernel,
        grid=(2 * half,),
        in_specs=[
            pl.BlockSpec((slots, tokens), lambda i: (0, 0)),
            pl.BlockSpec((slots, 1), lambda i: (0, 0)),
            pl.BlockSpec((tokens, block), lambda i: (0, jnp.minimum(i, half - 1))),
            pl.BlockSpec((tokens, block), lambda i: (0, jnp.maximum(i - half, 0))),
        ],
        out_specs=[spec, spec],
        out_shape=[out, out],
        compiler_params=limit(12),
        cost_estimate=cost(4 * slots * tokens * width, 8 * tokens * width),
    )(onehot, gate, inputs, upstream)


def forward_kernel(*refs):
    x_parts, dy_parts = refs[:5], refs[5:10]
    gate_ref, up_ref, down_ref = refs[10:13]
    x_ref, dy_ref, grads_ref, grads_t_ref, hidden_t_ref, prob_ref = refs[-9:-3]
    acc_g, acc_u, acc_b = refs[-3:]
    step = pl.program_id(0)

    @pl.when(step == 0)
    def _():
        acc_g[...] = jnp.zeros_like(acc_g)
        acc_u[...] = jnp.zeros_like(acc_u)
        acc_b[...] = jnp.zeros_like(acc_b)

    at = 0
    for x_part, dy_part in zip(x_parts, dy_parts):
        rows = x_part.shape[0]
        x_ref[at : at + rows, :] = x_part[...]
        dy_ref[at : at + rows, :] = dy_part[...]
        at += rows
    x = x_ref[...]
    acc_g[...] += dot(x, gate_ref[...])
    acc_u[...] += dot(x, up_ref[...])
    acc_b[...] += lax.dot_general(dy_ref[...], down_ref[...], BY_LAST, preferred_element_type=F32)

    @pl.when(step == pl.num_programs(0) - 1)
    def _():
        pre_gate, pre_up, back = acc_g[...], acc_u[...], acc_b[...]
        part = pre_gate.shape[1]
        sigma = jax.nn.sigmoid(pre_gate)
        act = pre_gate * sigma
        hidden = act * pre_up
        prob = jnp.sum(hidden * back, axis=1, keepdims=True)
        prob_ref[...] = jnp.broadcast_to(prob, prob_ref.shape).astype(BF)
        grad_g = back * pre_up * sigma * (1.0 + pre_gate * (1.0 - sigma))
        grad_u = back * act
        grads_ref[:, :part] = grad_g.astype(BF)
        grads_ref[:, part:] = grad_u.astype(BF)
        grads_t_ref[:part, :] = grad_g.T.astype(BF)
        grads_t_ref[part:, :] = grad_u.T.astype(BF)
        hidden_t_ref[...] = hidden.T.astype(BF)


def forward(parts, gate_w, up_w, down_w, after):
    width, part = gate_w.shape
    count = sum(p.shape[0] for p in parts)
    block = 1024
    steps = width // block
    return pl.pallas_call(
        forward_kernel,
        grid=(steps,),
        in_specs=[pl.BlockSpec((p.shape[0], block), lambda i: (0, i)) for p in parts]
        + [pl.BlockSpec((p.shape[0], block), lambda i: (0, i + steps)) for p in parts]
        + [
            pl.BlockSpec((block, part), lambda i: (i, 0)),
            pl.BlockSpec((block, part), lambda i: (i, 0)),
            pl.BlockSpec((part, block), lambda i: (0, i)),
        ]
        + [pl.BlockSpec(memory_space=pl.ANY)] * len(after),
        out_specs=[
            pl.BlockSpec((count, block), lambda i: (0, i)),
            pl.BlockSpec((count, block), lambda i: (0, i)),
            pl.BlockSpec((count, 2 * part), lambda i: (0, 0)),
            pl.BlockSpec((2 * part, count), lambda i: (0, 0)),
            pl.BlockSpec((part, count), lambda i: (0, 0)),
            pl.BlockSpec((count, LANES), lambda i: (0, 0)),
        ],
        out_shape=[
            jax.ShapeDtypeStruct((count, width), BF),
            jax.ShapeDtypeStruct((count, width), BF),
            jax.ShapeDtypeStruct((count, 2 * part), BF),
            jax.ShapeDtypeStruct((2 * part, count), BF),
            jax.ShapeDtypeStruct((part, count), BF),
            jax.ShapeDtypeStruct((count, LANES), BF),
        ],
        scratch_shapes=[pltpu.VMEM((count, part), F32)] * 3,
        compiler_params=limit(30),
        cost_estimate=cost(6 * count * width * part, 6 * width * part + 8 * count * width),
    )(*parts, *parts, gate_w, up_w, down_w, *after)


def weight_kernel(groups, outs, at_ref, *refs):
    x_refs, dy_refs = refs[:groups], refs[groups : 2 * groups]
    g_refs, h_refs = refs[2 * groups : 3 * groups], refs[3 * groups : 4 * groups]
    out_refs = refs[-outs:]
    top = sum(dot(g[...], x[...]) for g, x in zip(g_refs, x_refs)).astype(BF)
    low = sum(dot(h[...], d[...]) for h, d in zip(h_refs, dy_refs)).astype(BF)
    if outs == 1:
        out_refs[0][0, : top.shape[0], :] = top
        out_refs[0][0, top.shape[0] :, :] = low
    else:
        half = out_refs[0].shape[1]
        out_refs[0][0] = top[:half]
        out_refs[1][0, : top.shape[0] - half, :] = top[half:]
        out_refs[1][0, top.shape[0] - half :, :] = low


def weight_blocks(at, slice_w, xs, dys, grads_t, hiddens_t, outs, after=()):
    block = 512
    steps = slice_w // block
    count = at.shape[0]
    rows = grads_t[0].shape[0] + hiddens_t[0].shape[0]
    tall = [pl.BlockSpec((v.shape[0], block), lambda k, i, at: (0, at[k] * steps + i)) for v in xs]
    whole = [pl.BlockSpec(v.shape, lambda k, i, at: (0, 0)) for v in list(grads_t) + list(hiddens_t)]
    spec = pl.BlockSpec((1, rows // outs, block), lambda k, i, at: (k, 0, i))
    return pl.pallas_call(
        functools.partial(weight_kernel, len(xs), outs),
        grid_spec=pltpu.PrefetchScalarGridSpec(
            num_scalar_prefetch=1,
            grid=(count, steps),
            in_specs=tall + tall + whole + [pl.BlockSpec(memory_space=pl.ANY)] * len(after),
            out_specs=[spec] * outs,
        ),
        out_shape=[jax.ShapeDtypeStruct((count, rows // outs, slice_w), BF)] * outs,
        compiler_params=limit(20),
        cost_estimate=cost(count * 2 * rows * slice_w * sum(v.shape[0] for v in xs), count * 7 * MIB),
    )(at, *xs, *dys, *grads_t, *hiddens_t, *after)


def join_kernel(a_ref, b_ref, *refs):
    out_ref = refs[-1]
    rows = a_ref.shape[0]
    out_ref[:rows, :] = a_ref[...]
    out_ref[rows:, :] = b_ref[...]


def join_rows(a, b, after):
    block = 2048
    spec = pl.BlockSpec((a.shape[0], block), lambda i: (0, i))
    return pl.pallas_call(
        join_kernel,
        grid=(a.shape[1] // block,),
        in_specs=[spec, spec] + [pl.BlockSpec(memory_space=pl.ANY)] * len(after),
        out_specs=pl.BlockSpec((2 * a.shape[0], block), lambda i: (0, i)),
        out_shape=jax.ShapeDtypeStruct((2 * a.shape[0], a.shape[1]), BF),
        compiler_params=limit(8),
        cost_estimate=cost(0, 8 * a.size),
    )(a, b, *after)


def pass_kernel(*refs):
    pass


def order(value, after):
    spec = pl.BlockSpec(memory_space=pl.ANY)
    return pl.pallas_call(
        pass_kernel,
        in_specs=[spec] * (1 + len(after)),
        out_specs=spec,
        out_shape=jax.ShapeDtypeStruct(value.shape, value.dtype),
        input_output_aliases={0: 0},
        cost_estimate=cost(0, 0),
    )(value, *after)


def add_rows(a, b):
    return (a.astype(F32) + b.astype(F32)).astype(BF)


def dp_add_kernel(rest_ref, far_a_ref, far_b_ref, right_ref, left_ref):
    half = far_a_ref.shape[0]
    right_ref[:half, :] = add_rows(rest_ref[0, :half], far_a_ref[...])
    right_ref[half:, :] = rest_ref[0, half:]
    left_ref[:half, :] = rest_ref[1, :half]
    left_ref[half:, :] = add_rows(rest_ref[1, half:], far_b_ref[...])


def dp_add(rest, far_a, far_b):
    _, rows, width = rest.shape
    block = 256
    spec = pl.BlockSpec((rows // 2, block), lambda i: (0, i))
    out = pl.BlockSpec((rows, block), lambda i: (0, i))
    return pl.pallas_call(
        dp_add_kernel,
        grid=(width // block,),
        in_specs=[pl.BlockSpec((2, rows, block), lambda i: (0, 0, i)), spec, spec],
        out_specs=[out, out],
        out_shape=[jax.ShapeDtypeStruct((rows, width), BF)] * 2,
        compiler_params=limit(12),
        cost_estimate=cost(2 * rows * width, 10 * rows * width),
    )(rest, far_a, far_b)


def etp_add_kernel(left_ref, right_ref, far_a_ref, far_b_ref, *refs):
    left_out, right_out = refs[-2:]
    cut = far_a_ref.shape[0]
    right_out[:cut, :] = add_rows(right_ref[:cut], far_a_ref[...])
    right_out[cut:, :] = right_ref[cut:]
    left_out[:cut, :] = left_ref[:cut]
    left_out[cut:, :] = add_rows(left_ref[cut:], far_b_ref[...])


def etp_add(left, right, far_a, far_b, after):
    rows, width = left.shape
    block = 11 * LANES
    parts = (left, right, far_a, far_b)
    spec = pl.BlockSpec((rows, block), lambda i: (0, i))
    return pl.pallas_call(
        etp_add_kernel,
        grid=(width // block,),
        in_specs=[pl.BlockSpec((p.shape[0], block), lambda i: (0, i)) for p in parts]
        + [pl.BlockSpec(memory_space=pl.ANY)] * len(after),
        out_specs=[spec, spec],
        out_shape=[jax.ShapeDtypeStruct((rows, width), BF)] * 2,
        compiler_params=limit(12),
        cost_estimate=cost(rows * width, 10 * rows * width),
    )(*parts, *after)


def dx_kernel(sources, bands, *refs):
    grads, probs = refs[:sources], refs[sources : 2 * sources]
    gate_ref, up_ref = refs[2 * sources : 2 * sources + 2]
    out_refs, lhs, sums = refs[-len(bands) - 2 : -2], refs[-2], refs[-1]

    @pl.when(pl.program_id(0) == 0)
    def _():
        at = 0
        for grad, prob in zip(grads, probs):
            rows = grad.shape[0]
            lhs[at : at + rows, :] = grad[...]
            sums[at : at + rows, :] = prob[...]
            at += rows

    part = gate_ref.shape[1]
    total = lax.dot_general(lhs[:, :part], gate_ref[...], BY_LAST, preferred_element_type=F32)
    total += lax.dot_general(lhs[:, part:], up_ref[...], BY_LAST, preferred_element_type=F32)
    total = total.astype(BF)
    for out, band in zip(out_refs, bands):
        to = 0
        for at, rows in band:
            out[to : to + rows, :] = total[at : at + rows]
            to += rows

    @pl.when(pl.program_id(0) == pl.num_programs(0) - 1)
    def _():
        for out, band in zip(out_refs, bands):
            to = 0
            for at, rows in band:
                out[to : to + rows, out.shape[1] - LANES :] = sums[at : at + rows, :]
                to += rows


def dx_blocks(grads, probs, gate_w, up_w, bands, after):
    width, part = gate_w.shape
    count = sum(g.shape[0] for g in grads)
    block = 11 * LANES
    steps = (width + LANES) // block
    sizes = [sum(rows for _, rows in band) for band in bands]
    return pl.pallas_call(
        functools.partial(dx_kernel, len(grads), bands),
        grid=(steps,),
        in_specs=[pl.BlockSpec(v.shape, lambda i: (0, 0)) for v in (*grads, *probs)]
        + [pl.BlockSpec((block, part), lambda i: (i, 0))] * 2
        + [pl.BlockSpec(memory_space=pl.ANY)] * len(after),
        out_specs=[pl.BlockSpec((rows, block), lambda i: (0, i)) for rows in sizes],
        out_shape=[jax.ShapeDtypeStruct((rows, width + LANES), BF) for rows in sizes],
        scratch_shapes=[pltpu.VMEM((count, 2 * part), BF), pltpu.VMEM((count, LANES), BF)],
        compiler_params=limit(30),
        cost_estimate=cost(4 * count * width * part, 4 * width * part + 2 * count * width),
    )(*grads, *probs, gate_w, up_w, *after)


def final_kernel(own_ref, left_ref, right_ref, gate_ref, up_ref, down_ref):
    total = own_ref[0].astype(F32) + left_ref[...].astype(F32) + right_ref[...].astype(F32)
    part = down_ref.shape[0]
    gate_ref[...] = total[:part].T.astype(BF)
    up_ref[...] = total[part : 2 * part].T.astype(BF)
    down_ref[...] = total[2 * part :].astype(BF)


def final_sum(rest, left, right):
    rows, width = left.shape
    part = rows // 3
    block = 256
    spec = pl.BlockSpec((rows, block), lambda i: (0, i))
    tall = pl.BlockSpec((block, part), lambda i: (i, 0))
    return pl.pallas_call(
        final_kernel,
        grid=(width // block,),
        in_specs=[pl.BlockSpec((1, rows, block), lambda i: (2, 0, i)), spec, spec],
        out_specs=[tall, tall, pl.BlockSpec((part, block), lambda i: (0, i))],
        out_shape=[jax.ShapeDtypeStruct((width, part), BF)] * 2 + [jax.ShapeDtypeStruct((part, width), BF)],
        compiler_params=limit(16),
        cost_estimate=cost(rows * width, 8 * rows * width),
    )(rest, left, right)


def split_band(band, size):
    first, second = [], []
    for at, rows in band:
        take = min(rows, size)
        if take:
            first.append((at, take))
        if rows > take:
            second.append((at + take, rows - take))
        size -= take
    return [first, second]


def ring(axis):
    size = lax.axis_size(axis)
    return [(i, (i + 1) % size) for i in range(size)], [(i, (i - 1) % size) for i in range(size)]


def ring_gather(block, axis, cut, after=()):
    to_right, to_left = ring(axis)
    left = lax.ppermute(block, axis, to_right)
    right = lax.ppermute(block, axis, to_left)
    if after:
        left, right = order(left, after), order(right, after)
    far_a = lax.ppermute(left[:cut], axis, to_right)
    far_b = lax.ppermute(right[cut:], axis, to_left)
    return [block, left, right, far_a, far_b]


def ring_first(far_a, far_b, axis):
    to_right, to_left = ring(axis)
    return lax.ppermute(far_a, axis, to_right), lax.ppermute(far_b, axis, to_left)


def ring_second(left, right, axis):
    to_right, to_left = ring(axis)
    return lax.ppermute(right, axis, to_right), lax.ppermute(left, axis, to_left)


def body(inputs, upstream, experts, gate_probs, gate_weight, up_weight, down_weight):
    experts_n = lax.axis_size("ep")
    layers = experts_n // 2
    width = inputs.shape[1]
    me = lax.axis_index("ep")
    z, core = me // 2, me % 2
    expert_ids = jnp.stack(
        [2 * ((z + dz) % layers) + (core ^ dc) for dc in range(2) for dz in range(layers)]
    ).astype(jnp.int32)
    swap = [(2 * i + j, 2 * i + 1 - j) for i in range(layers) for j in range(2)]

    def shift(dz):
        return [(2 * i + j, 2 * ((i + dz) % layers) + j) for i in range(layers) for j in range(2)]

    onehot, chosen, slot_gate = slot_tables(experts, gate_probs, expert_ids, CAP)
    slots = experts_n * CAP
    pick = onehot.astype(BF).reshape(slots, -1)
    gate = slot_gate.astype(BF).astype(F32).reshape(slots, 1)
    mine, others = pick_rows(pick, gate, inputs, upstream)
    others = lax.ppermute(others, "ep", swap)

    gate_w, up_w, down_w = gate_weight[0], up_weight[0], down_weight[0]
    blocks = {}
    for dz in range(layers):
        at = slice(dz * CAP, (dz + 1) * CAP)
        block = jnp.concatenate([mine[at], others[at]])
        if dz == 2:
            block = order(block, (blocks[1],))
        blocks[dz] = lax.ppermute(block, "ep", shift(dz)) if dz else block
    groups = [(0,), (1, 3), (2,)]
    cuts = [32, 48, 16]
    xs, dys, grads, grads_t, hiddens_t, probs = [], [], [], [], [], []
    parts = [None] * len(groups)
    for i, (group, cut) in enumerate(zip(groups, cuts)):
        after = ()
        if i == 1:
            block = join_rows(blocks[group[0]], blocks[group[1]], tuple(parts[0][1:3]))
        elif i == 2:
            block = order(blocks[group[0]], tuple(parts[1][1:3] + parts[0][3:]))
            after = (probs[0], *parts[1][3:])
        else:
            block = blocks[group[0]]
        parts[i] = ring_gather(block, "etp", cut, after)
        results = forward(parts[i], gate_w, up_w, down_w, probs[-1:])
        for kept, result in zip((xs, dys, grads, grads_t, hiddens_t, probs), results):
            kept.append(result)

    dp = lax.axis_size("dp")
    slice_w = width // dp
    my_dp = lax.axis_index("dp")

    def weights_for(ahead, outs, after=()):
        at = jnp.stack([(my_dp + k) % dp for k in ahead]).astype(jnp.int32)
        return weight_blocks(at, slice_w, xs, dys, grads_t, hiddens_t, outs, after)

    far_a, far_b = weights_for((2,), 2)
    got_wa, got_wb = ring_first(far_a[0], far_b[0], "dp")

    step = 2 * CAP
    plans = [
        ((1, 2), (1, 3, 2), [(0, 2 * step), (8 * step, step)], 80, 64),
        ((0,), (0,), [(0, step)], 16, 32),
    ]
    pieces, got = [], []
    after = (far_a,)
    for sources, members, firsts, size_a, size_b in plans:
        bands = [[(at + k * rows, rows) for at, rows in firsts] for k in range(3)]
        far = [(at + 3 * rows, rows) for at, rows in firsts]
        bands += split_band(far, size_a)
        out = dx_blocks([grads[k] for k in sources], [probs[k] for k in sources], gate_w, up_w, bands, after)
        pieces.append(out)
        got.append(ring_first(out[3], out[4], "etp"))
        after = (out[0],)

    (rest,) = weights_for((1, dp - 1, 0), 1, after)
    right_w, left_w = dp_add(rest, got_wa, got_wb)
    from_left_w, from_right_w = ring_second(left_w, right_w, "dp")

    returned = {}
    for (sources, members, *_), out, far in zip(plans, pieces, got):
        own, left, right = out[:3]
        left, right = etp_add(left, right, *far, (right_w,))
        from_left, from_right = ring_second(left, right, "etp")
        total = (own.astype(F32) + from_left.astype(F32) + from_right.astype(F32)).astype(BF)
        for i, dz in enumerate(members):
            block = total[i * step : (i + 1) * step]
            returned[dz] = lax.ppermute(block, "ep", shift(layers - dz)) if dz else block
    mine_rows = jnp.concatenate([returned[dz][:CAP] for dz in range(layers)])
    others = jnp.concatenate([returned[dz][CAP:] for dz in range(layers)])
    others = lax.ppermute(others, "ep", swap)
    dx_slots = jnp.concatenate([mine_rows, others])
    grad_inputs = lax.dot_general(pick, dx_slots[:, :width], BY_FIRST, preferred_element_type=F32).astype(BF)
    prob_sum = dx_slots[:, width].astype(F32).reshape(experts_n, CAP)
    gates = gate.reshape(experts_n, CAP)
    prob_slots = (prob_sum / jnp.where(gates > 0, gates, 1.0)).astype(BF).astype(F32)
    per_expert = jnp.sum(jnp.where(onehot, prob_slots[:, :, None], 0.0), axis=1)
    grad_probs = jnp.sum(jnp.where(chosen, per_expert.T[:, None, :], 0.0), axis=2)

    grad_gate, grad_up, grad_down = final_sum(rest, from_left_w, from_right_w)
    return (grad_inputs, grad_probs, grad_gate[None], grad_up[None], grad_down[None])


def solution(mesh):
    tokens = P(("ep", "etp", "dp"), None)
    return jax.shard_map(
        body,
        mesh=mesh,
        in_specs=(tokens, tokens, tokens, tokens, P("ep", None, "etp"), P("ep", None, "etp"), P("ep", "etp", None)),
        out_specs=(tokens, tokens, P("ep", "dp", "etp"), P("ep", "dp", "etp"), P("ep", "etp", "dp")),
        check_vma=False,
    )
```

profile of v0, /device:TPU:0, one launch (start us, length us, event | category | flops | bytes accessed | tf_op | source)
XLA Modules:
  0.0 264.1 jit_solution(8092528726467187267)
XLA Ops:
  7.6 2.9 %shard_map.110 = (bf16[96,8192]{1,0:T(8,128)(2,1)S(1)}, bf16[96,8192]{1,0:T(8,128)(2,1)S(1)}) custom-call(bf16[192,256]{1,0:T(8,128)(2,1)S(1)} %get-tuple-element.106.onehot_ref, f32[192,1]{1,0:T(8,128)S(1)} %reshape.77.gate_ref, bf16[256,4096]{1,0:T(8,128)(2,1)S(1)} %copy-done.35, bf16[256,4096]{1,0:T(8,128)(2,1)S(1)} %copy-done.36), custom_call_target="tpu_custom_call" | custom-call | flops 805306368 | bytes 8388608 | tf_op jit(solution)/shard_map/pallas_call | solution.py:68
  10.7 3.3 %collective-permute-done = bf16[96,8192]{1,0:T(8,128)(2,1)S(1)} collective-permute-done((bf16[96,8192]{1,0:T(8,128)(2,1)S(1)}, bf16[96,8192]{1,0:T(8,128)(2,1)S(1)}, u32[]{:S(2)}, u32[]{:S(2)}) %collective-permute-start) | collective-permute-done | bytes 1572896 | tf_op jit(solution)/shard_map/ppermute | solution.py:428
  16.3 2.2 collective-permute-start.6
  18.6 3.1 %collective-permute-start.2 = (bf16[48,8192]{1,0:T(8,128)(2,1)S(1)}, bf16[48,8192]{1,0:T(8,128)(2,1)S(1)}, u32[]{:S(2)}, u32[]{:S(2)}) collective-permute-start(bf16[48,8192]{1,0:T(8,128)(2,1)S(1)} %pad_maximum_fusion.1.refs_0_.refs_5_), channel_id=1, source_target_pairs={{0,12},{4,0},{8,4},{12,8},{1,13},{5,1},{9,5},{13,9},{2,14},{6,2},{... | collective-permute-start | bytes 2359304 | tf_op jit(solution)/shard_map/ppermute | solution.py:391
  21.7 14.5 %collective-permute-done.5.a_ref.refs_1_ = bf16[48,8192]{1,0:T(8,128)(2,1)S(1)} collective-permute-done((bf16[48,8192]{1,0:T(8,128)(2,1)S(1)}, bf16[48,8192]{1,0:T(8,128)(2,1)S(1)}, u32[]{:S(2)}, u32[]{:S(2)}) %collective-permute-start.5) | collective-permute-done | bytes 786464 | tf_op jit(solution)/shard_map/ppermute | solution.py:437
  36.2 2.3 collective-permute-done.2.refs_2_.refs_7_.refs_1_
  38.5 3.4 %collective-permute-done.1.refs_1_.refs_6_.refs_0_ = bf16[48,8192]{1,0:T(8,128)(2,1)S(1)} collective-permute-done((bf16[48,8192]{1,0:T(8,128)(2,1)S(1)}, bf16[48,8192]{1,0:T(8,128)(2,1)S(1)}, u32[]{:S(2)}, u32[]{:S(2)}) %collective-permute-start.1) | collective-permute-done | bytes 786464 | tf_op jit(solution)/shard_map/ppermute | solution.py:390
  50.6 3.3 %collective-permute-start.4 = (bf16[16,8192]{1,0:T(8,128)(2,1)S(1)}, bf16[16,8192]{1,0:T(8,128)(2,1)S(1)}, u32[]{:S(2)}, u32[]{:S(2)}) collective-permute-start(bf16[16,8192]{1,0:T(8,128)(2,1)S(1)} %slice.119), channel_id=1, source_target_pairs={{0,12},{4,0},{8,4},{12,8},{1,13},{5,1},{9,5},{13,9},{2,14},{6,2},{... | collective-permute-start | bytes 786440 | tf_op jit(solution)/shard_map/ppermute | solution.py:395
  53.9 27.5 %collective-permute-done.8.refs_2_.refs_7_ = bf16[96,8192]{1,0:T(8,128)(2,1)S(1)} collective-permute-done((bf16[96,8192]{1,0:T(8,128)(2,1)}, bf16[96,8192]{1,0:T(8,128)(2,1)S(1)}, u32[]{:S(2)}, u32[]{:S(2)}) %collective-permute-start.8) | collective-permute-done | bytes 1572896 | tf_op jit(solution)/shard_map/ppermute | solution.py:391
  87.1 7.2 %collective-permute-done.3.refs_3_.refs_8_ = bf16[32,8192]{1,0:T(8,128)(2,1)} collective-permute-done((bf16[32,8192]{1,0:T(8,128)(2,1)S(1)}, bf16[32,8192]{1,0:T(8,128)(2,1)}, u32[]{:S(2)}, u32[]{:S(2)}) %collective-permute-start.3) | collective-permute-done | bytes 524320 | tf_op jit(solution)/shard_map/ppermute | solution.py:394
  104.5 5.3 %shard_map.111 = (bf16[192,4096]{1,0:T(8,128)(2,1)S(1)}, bf16[192,4096]{1,0:T(8,128)(2,1)S(1)}, bf16[192,768]{1,0:T(8,128)(2,1)S(1)}, bf16[768,192]{1,0:T(8,128)...) custom-call(bf16[48,8192]{1,0:T(8,128)(2,1)S(1)} %copy-done.19, bf16[48,8192]{1,0:T(8,128)(2,1)S(1)} %copy-done.15, ...), custom_call_target="tpu_custom_call" | custom-call | flops 1811939328 | bytes 15728640 | tf_op jit(solution)/shard_map/pallas_call | solution.py:131
  114.2 4.3 %collective-permute-done.13.refs_0_ = bf16[48,8192]{1,0:T(8,128)(2,1)} collective-permute-done((bf16[48,8192]{1,0:T(8,128)(2,1)}, bf16[48,8192]{1,0:T(8,128)(2,1)}, u32[]{:S(2)}, u32[]{:S(2)}) %collective-permute-start.13) | collective-permute-done | bytes 786464 | tf_op jit(solution)/shard_map/ppermute | solution.py:391
  122.2 3.5 %collective-permute-done.12.refs_0_ = bf16[48,8192]{1,0:T(8,128)(2,1)} collective-permute-done((bf16[48,8192]{1,0:T(8,128)(2,1)}, bf16[48,8192]{1,0:T(8,128)(2,1)}, u32[]{:S(2)}, u32[]{:S(2)}) %collective-permute-start.12) | collective-permute-done | bytes 786464 | tf_op jit(solution)/shard_map/ppermute | solution.py:390
  134.5 8.4 %shard_map.113 = (bf16[384,4096]{1,0:T(8,128)(2,1)S(1)}, bf16[384,4096]{1,0:T(8,128)(2,1)S(1)}, bf16[384,768]{1,0:T(8,128)(2,1)S(1)}, bf16[768,384]{1,0:T(8,128)...) custom-call(bf16[96,8192]{1,0:T(8,128)(2,1)} %shard_map.112.refs_0_.refs_5_, ...), custom_call_target="tpu_custom_call" | custom-call | flops 3623878656 | bytes 22020096 | tf_op jit(solution)/shard_map/pallas_call | solution.py:131
  143.8 7.5 %shard_map.118 = (bf16[192,4096]{1,0:T(8,128)(2,1)S(1)}, bf16[192,4096]{1,0:T(8,128)(2,1)S(1)}, bf16[192,768]{1,0:T(8,128)(2,1)S(1)}, bf16[768,192]{1,0:T(8,128)...) custom-call(bf16[48,8192]{1,0:T(8,128)(2,1)} %shard_map.115.refs_0_.refs_5_, ...), custom_call_target="tpu_custom_call" | custom-call | flops 1811939328 | bytes 15728640 | tf_op jit(solution)/shard_map/pallas_call | solution.py:131
  151.4 4.0 %shard_map.119 = (bf16[1,576,1024]{2,1,0:T(8,128)(2,1)}, bf16[1,576,1024]{2,1,0:T(8,128)(2,1)}) custom-call(s32[1]{0:T(128)} %bitcast.17.at_ref, bf16[192,4096]{1,0:T(8,128)(2,1)S(1)} %copy-done.21, bf16[384,4096]{1,0:T(8,128)(2,1)S(1)} %get-tuple-element.55.refs_1_, bf16[192,4096]{1,0:T(8,128)(2,1)S(1)} %get-tuple-element.56.refs_2_, ...), custom_call_target="tpu_custom_call" | custom-call | flops 1811939328 | bytes 7340032 | tf_op jit(solution)/shard_map/pallas_call | solution.py:188
  164.5 6.4 %shard_map.120 = (bf16[144,4224]{1,0:T(8,128)(2,1)S(1)}, bf16[144,4224]{1,0:T(8,128)(2,1)S(1)}, bf16[144,4224]{1,0:T(8,128)(2,1)S(1)}, bf16[80,4224]{1,0:T(8,128)(2,1)S(1)}, bf16[64,4224]{1,0:T(8,128)(2,1)S(1)}) custom-call(bf16[384,768]{1,0:T(8,128)(2,1)S(1)} %copy-done.54, bf16[192,768]{1,0:T(8,128)(2,1)S(1)} %copy-done.56, ...), custom_call_target="tpu_custom_call" | custom-call | flops 3623878656 | bytes 11010048 | tf_op jit(solution)/shard_map/pallas_call | solution.py:332
  170.9 3.1 %collective-permute-start.23 = (bf16[64,4224]{1,0:T(8,128)(2,1)S(1)}, bf16[64,4224]{1,0:T(8,128)(2,1)S(1)}, u32[]{:S(2)}, u32[]{:S(2)}) collective-permute-start(bf16[64,4224]{1,0:T(8,128)(2,1)S(1)} %get-tuple-element.80), channel_id=1, source_target_pairs={{0,12},{4,0},{8,4},{12,8},{1,13},{5,1},{9,5},{13,9},{2,14},{6,2},{... | collective-permute-start | bytes 1622024 | tf_op jit(solution)/shard_map/ppermute | solution.py:401
  174.1 2.9 %shard_map.121 = (bf16[48,4224]{1,0:T(8,128)(2,1)S(1)}, bf16[48,4224]{1,0:T(8,128)(2,1)S(1)}, bf16[48,4224]{1,0:T(8,128)(2,1)S(1)}, bf16[16,4224]{1,0:T(8,128)(2,1)S(1)}, bf16[32,4224]{1,0:T(8,128)(2,1)S(1)}) custom-call(bf16[192,768]{1,0:T(8,128)(2,1)S(1)} %copy-done.50, bf16[192,128]{1,0:T(8,128)(2,1)S(1)} %copy-done.48, bf16[4096,384]{1,0:T(8,128)(2,1)S(1)} %bitcast.43, ...), custom_call_target="tpu_custom_call" | custom-call | flops 1207959552 | bytes 7864320 | tf_op jit(solution)/shard_map/pallas_call | solution.py:332
  177.1 5.5 %collective-permute-done.18.far_a_ref = bf16[576,1024]{1,0:T(8,128)(2,1)} collective-permute-done((bf16[576,1024]{1,0:T(8,128)(2,1)}, bf16[576,1024]{1,0:T(8,128)(2,1)}, u32[]{:S(2)}, u32[]{:S(2)}) %collective-permute-start.18) | collective-permute-done | bytes 1179680 | tf_op jit(solution)/shard_map/ppermute | solution.py:401
  182.6 2.9 %collective-permute-start.17 = (bf16[32,4224]{1,0:T(8,128)(2,1)S(1)}, bf16[32,4224]{1,0:T(8,128)(2,1)S(1)}, u32[]{:S(2)}, u32[]{:S(2)}) collective-permute-start(bf16[32,4224]{1,0:T(8,128)(2,1)S(1)} %get-tuple-element.72), channel_id=1, source_target_pairs={{0,12},{4,0},{8,4},{12,8},{1,13},{5,1},{9,5},{13,9},{2,14},{6,2},{... | collective-permute-start | bytes 811016 | tf_op jit(solution)/shard_map/ppermute | solution.py:401
  185.6 10.5 %shard_map.122.rest_ref.own_ref = bf16[3,1152,1024]{2,1,0:T(8,128)(2,1)S(1)} custom-call(s32[3]{0:T(128)S(1)} %pad_add_fusion.at_ref, bf16[192,4096]{1,0:T(8,128)(2,1)S(1)} %copy-done.22, bf16[384,4096]{1,0:T(8,128)(2,1)S(1)} %copy-done.11, bf16[192,4096]{1,0:T(8,128)(2,1)S(1)} %copy-done.27, bf16[192,4096]{1,0:T(8,128)(2,1)S(1)} %copy-done.25, ...), custom_call_target="tpu_custom_call" | custom-call | flops 5435817984 | bytes 22020096 | tf_op jit(solution)/shard_map/pallas_call | solution.py:188
  196.1 3.6 %shard_map.123 = (bf16[1152,1024]{1,0:T(8,128)(2,1)S(1)}, bf16[1152,1024]{1,0:T(8,128)(2,1)S(1)}) custom-call(bf16[3,1152,1024]{2,1,0:T(8,128)(2,1)S(1)} %shard_map.122.rest_ref.own_ref, bf16[576,1024]{1,0:T(8,128)(2,1)} %collective-permute-done.18.far_a_ref, bf16[576,1024]{1,0:T(8,128)(2,1)} %collective-permute-done.19.far_b_ref), custom_call_target="tpu_custom_call" | custom-call | flops 2359296 | bytes 11796480 | tf_op jit(solution)/shard_map/pallas_call | solution.py:256
  200.2 3.2 %collective-permute-start.21 = (bf16[48,4224]{1,0:T(8,128)(2,1)S(1)}, bf16[48,4224]{1,0:T(8,128)(2,1)S(1)}, u32[]{:S(2)}, u32[]{:S(2)}) collective-permute-start(bf16[48,4224]{1,0:T(8,128)(2,1)S(1)} %get-tuple-element.76), channel_id=1, source_target_pairs={{0,12},{4,0},{8,4},{12,8},{1,13},{5,1},{9,5},{13,9},{2,14},{6,2},{... | collective-permute-start | bytes 1216520 | tf_op jit(solution)/shard_map/ppermute | solution.py:406
  204.3 3.2 %collective-permute-start.25 = (bf16[144,4224]{1,0:T(8,128)(2,1)S(1)}, bf16[144,4224]{1,0:T(8,128)(2,1)S(1)}, u32[]{:S(2)}, u32[]{:S(2)}) collective-permute-start(bf16[144,4224]{1,0:T(8,128)(2,1)S(1)} %get-tuple-element.82), channel_id=1, source_target_pairs={{0,12},{4,0},{8,4},{12,8},{1,13},{5,1},{9,5},{13,9},{2,14},{6,2},{... | collective-permute-start | bytes 3649544 | tf_op jit(solution)/shard_map/ppermute | solution.py:406
  207.9 5.8 %collective-permute-done.20 = bf16[48,4224]{1,0:T(8,128)(2,1)S(1)} collective-permute-done((bf16[48,4224]{1,0:T(8,128)(2,1)S(1)}, bf16[48,4224]{1,0:T(8,128)(2,1)S(1)}, u32[]{:S(2)}, u32[]{:S(2)}) %collective-permute-start.20) | collective-permute-done | bytes 405536 | tf_op jit(solution)/shard_map/ppermute | solution.py:406
  215.4 19.6 %collective-permute-done.24 = bf16[144,4224]{1,0:T(8,128)(2,1)S(1)} collective-permute-done((bf16[144,4224]{1,0:T(8,128)(2,1)S(1)}, bf16[144,4224]{1,0:T(8,128)(2,1)S(1)}, u32[]{:S(2)}, u32[]{:S(2)}) %collective-permute-start.24) | collective-permute-done | bytes 1216544 | tf_op jit(solution)/shard_map/ppermute | solution.py:406
  238.4 8.3 %collective-permute-done.26 = bf16[48,4224]{1,0:T(8,128)(2,1)S(1)} collective-permute-done((bf16[48,4224]{1,0:T(8,128)(2,1)S(1)}, bf16[48,4224]{1,0:T(8,128)(2,1)S(1)}, u32[]{:S(2)}, u32[]{:S(2)}) %collective-permute-start.26) | collective-permute-done | bytes 405536 | tf_op jit(solution)/shard_map/ppermute | solution.py:495
  246.8 4.5 %collective-permute-done.27 = bf16[48,4224]{1,0:T(8,128)(2,1)S(1)} collective-permute-done((bf16[48,4224]{1,0:T(8,128)(2,1)S(1)}, bf16[48,4224]{1,0:T(8,128)(2,1)S(1)}, u32[]{:S(2)}, u32[]{:S(2)}) %collective-permute-start.27) | collective-permute-done | bytes 405536 | tf_op jit(solution)/shard_map/ppermute | solution.py:495
  252.7 4.9 %collective-permute-done.31.right_ref = bf16[1152,1024]{1,0:T(8,128)(2,1)S(1)} collective-permute-done((bf16[1152,1024]{1,0:T(8,128)(2,1)S(1)}, bf16[1152,1024]{1,0:T(8,128)(2,1)S(1)}, u32[]{:S(2)}, u32[]{:S(2)}) %collective-permute-start.31) | collective-permute-done | bytes 2359328 | tf_op jit(solution)/shard_map/ppermute | solution.py:406
  257.6 3.1 %shard_map.126 = (bf16[1024,384]{1,0:T(8,128)(2,1)}, bf16[1024,384]{1,0:T(8,128)(2,1)}, bf16[384,1024]{1,0:T(8,128)(2,1)}) custom-call(bf16[3,1152,1024]{2,1,0:T(8,128)(2,1)S(1)} %shard_map.122.rest_ref.own_ref, bf16[1152,1024]{1,0:T(8,128)(2,1)S(1)} %collective-permute-done.30.left_ref, bf16[1152,1024]{1,0:T(8,128)(2,1)S(1)} %collective-permute-done.31.right_ref), custom_call_target="tpu_custom_call" | custom-call | flops 1179648 | bytes 9437184 | tf_op jit(solution)/shard_map/pallas_call | solution.py:360
  262.1 2.1 convolution_convert_fusion
  (217 shorter events, 70.3 us)
Async XLA Ops:
  10.5 3.5 %collective-permute-start = (bf16[96,8192]{1,0:T(8,128)(2,1)S(1)}, bf16[96,8192]{1,0:T(8,128)(2,1)S(1)}, u32[]{:S(2)}, u32[]{:S(2)}) collective-permute-start(bf16[96,8192]{1,0:T(8,128)(2,1)S(1)} %get-tuple-element.47), channel_id=1, source_target_pairs={{0,16},{16,0},{32,48},{48,32},{64,80},{80,64},{96,112},{112,96},{1... | collective-permute-start | bytes 4718600 | tf_op jit(solution)/shard_map/ppermute | solution.py:428
  14.2 22.0 %collective-permute-start.5 = (bf16[48,8192]{1,0:T(8,128)(2,1)S(1)}, bf16[48,8192]{1,0:T(8,128)(2,1)S(1)}, u32[]{:S(2)}, u32[]{:S(2)}) collective-permute-start(bf16[48,8192]{1,0:T(8,128)(2,1)S(1)} %pad_maximum_fusion.2), channel_id=1, source_target_pairs={{0,32},{16,48},{32,64},{48,80},{64,96},{80,112},{96,0},{112,16},{1... | collective-permute-start | bytes 2359304 | tf_op jit(solution)/shard_map/ppermute | solution.py:437
  16.3 19.9 %collective-permute-start.6 = (bf16[48,8192]{1,0:T(8,128)(2,1)S(1)}, bf16[48,8192]{1,0:T(8,128)(2,1)S(1)}, u32[]{:S(2)}, u32[]{:S(2)}) collective-permute-start(bf16[48,8192]{1,0:T(8,128)(2,1)S(1)} %pad_maximum_fusion.3), channel_id=1, source_target_pairs={{0,96},{16,112},{32,0},{48,16},{64,32},{80,48},{96,64},{112,80},{1... | collective-permute-start | bytes 2359304 | tf_op jit(solution)/shard_map/ppermute | solution.py:437
  18.6 19.9 %collective-permute-start.2 = (bf16[48,8192]{1,0:T(8,128)(2,1)S(1)}, bf16[48,8192]{1,0:T(8,128)(2,1)S(1)}, u32[]{:S(2)}, u32[]{:S(2)}) collective-permute-start(bf16[48,8192]{1,0:T(8,128)(2,1)S(1)} %pad_maximum_fusion.1.refs_0_.refs_5_), channel_id=1, source_target_pairs={{0,12},{4,0},{8,4},{12,8},{1,13},{5,1},{9,5},{13,9},{2,14},{6,2},{... | collective-permute-start | bytes 2359304 | tf_op jit(solution)/shard_map/ppermute | solution.py:391
  21.7 20.2 %collective-permute-start.1 = (bf16[48,8192]{1,0:T(8,128)(2,1)S(1)}, bf16[48,8192]{1,0:T(8,128)(2,1)S(1)}, u32[]{:S(2)}, u32[]{:S(2)}) collective-permute-start(bf16[48,8192]{1,0:T(8,128)(2,1)S(1)} %pad_maximum_fusion.1.refs_0_.refs_5_), channel_id=1, source_target_pairs={{0,4},{4,8},{8,12},{12,0},{1,5},{5,9},{9,13},{13,1},{2,6},{6,10},{... | collective-permute-start | bytes 2359304 | tf_op jit(solution)/shard_map/ppermute | solution.py:390
  43.8 37.6 %collective-permute-start.8 = (bf16[96,8192]{1,0:T(8,128)(2,1)}, bf16[96,8192]{1,0:T(8,128)(2,1)S(1)}, u32[]{:S(2)}, u32[]{:S(2)}) collective-permute-start(bf16[96,8192]{1,0:T(8,128)(2,1)} %shard_map.112.refs_0_.refs_5_), channel_id=1, source_target_pairs={{0,12},{4,0},{8,4},{12,8},{1,13},{5,1},{9,5},{13,9},{2,14},{6,2},{... | collective-permute-start | bytes 4718600 | tf_op jit(solution)/shard_map/ppermute | solution.py:391
  44.2 39.8 %collective-permute-start.7 = (bf16[96,8192]{1,0:T(8,128)(2,1)}, bf16[96,8192]{1,0:T(8,128)(2,1)S(1)}, u32[]{:S(2)}, u32[]{:S(2)}) collective-permute-start(bf16[96,8192]{1,0:T(8,128)(2,1)} %shard_map.112.refs_0_.refs_5_), channel_id=1, source_target_pairs={{0,4},{4,8},{8,12},{12,0},{1,5},{5,9},{9,13},{13,1},{2,6},{6,10},{... | collective-permute-start | bytes 4718600 | tf_op jit(solution)/shard_map/ppermute | solution.py:390
  46.9 47.4 %collective-permute-start.11 = (bf16[48,8192]{1,0:T(8,128)(2,1)}, bf16[48,8192]{1,0:T(8,128)(2,1)}, u32[]{:S(2)}, u32[]{:S(2)}) collective-permute-start(bf16[48,8192]{1,0:T(8,128)(2,1)} %shard_map.114), channel_id=1, source_target_pairs={{0,64},{16,80},{32,96},{48,112},{64,0},{80,16},{96,32},{112,48},{1... | collective-permute-start | bytes 2359304 | tf_op jit(solution)/shard_map/ppermute | solution.py:437
  49.6 44.7 %collective-permute-start.3 = (bf16[32,8192]{1,0:T(8,128)(2,1)S(1)}, bf16[32,8192]{1,0:T(8,128)(2,1)}, u32[]{:S(2)}, u32[]{:S(2)}) collective-permute-start(bf16[32,8192]{1,0:T(8,128)(2,1)S(1)} %slice.118), channel_id=1, source_target_pairs={{0,4},{4,8},{8,12},{12,0},{1,5},{5,9},{9,13},{13,1},{2,6},{6,10},{... | collective-permute-start | bytes 1572872 | tf_op jit(solution)/shard_map/ppermute | solution.py:394
  50.6 36.4 %collective-permute-start.4 = (bf16[16,8192]{1,0:T(8,128)(2,1)S(1)}, bf16[16,8192]{1,0:T(8,128)(2,1)S(1)}, u32[]{:S(2)}, u32[]{:S(2)}) collective-permute-start(bf16[16,8192]{1,0:T(8,128)(2,1)S(1)} %slice.119), channel_id=1, source_target_pairs={{0,12},{4,0},{8,4},{12,8},{1,13},{5,1},{9,5},{13,9},{2,14},{6,2},{... | collective-permute-start | bytes 786440 | tf_op jit(solution)/shard_map/ppermute | solution.py:395
  82.4 31.7 %collective-permute-start.10 = (bf16[48,8192]{1,0:T(8,128)(2,1)}, bf16[48,8192]{1,0:T(8,128)(2,1)}, u32[]{:S(2)}, u32[]{:S(2)}) collective-permute-start(bf16[48,8192]{1,0:T(8,128)(2,1)} %slice.123), channel_id=1, source_target_pairs={{0,12},{4,0},{8,4},{12,8},{1,13},{5,1},{9,5},{13,9},{2,14},{6,2},{... | collective-permute-start | bytes 2359304 | tf_op jit(solution)/shard_map/ppermute | solution.py:395
  86.0 28.1 %collective-permute-start.9 = (bf16[48,8192]{1,0:T(8,128)(2,1)}, bf16[48,8192]{1,0:T(8,128)(2,1)}, u32[]{:S(2)}, u32[]{:S(2)}) collective-permute-start(bf16[48,8192]{1,0:T(8,128)(2,1)} %slice.122), channel_id=1, source_target_pairs={{0,4},{4,8},{8,12},{12,0},{1,5},{5,9},{9,13},{13,1},{2,6},{6,10},{... | collective-permute-start | bytes 2359304 | tf_op jit(solution)/shard_map/ppermute | solution.py:394
  94.3 24.2 %collective-permute-start.13 = (bf16[48,8192]{1,0:T(8,128)(2,1)}, bf16[48,8192]{1,0:T(8,128)(2,1)}, u32[]{:S(2)}, u32[]{:S(2)}) collective-permute-start(bf16[48,8192]{1,0:T(8,128)(2,1)} %shard_map.115.refs_0_.refs_5_), channel_id=1, source_target_pairs={{0,12},{4,0},{8,4},{12,8},{1,13},{5,1},{9,5},{13,9},{2,14},{6,2},{... | collective-permute-start | bytes 2359304 | tf_op jit(solution)/shard_map/ppermute | solution.py:391
  94.3 31.4 %collective-permute-start.12 = (bf16[48,8192]{1,0:T(8,128)(2,1)}, bf16[48,8192]{1,0:T(8,128)(2,1)}, u32[]{:S(2)}, u32[]{:S(2)}) collective-permute-start(bf16[48,8192]{1,0:T(8,128)(2,1)} %shard_map.115.refs_0_.refs_5_), channel_id=1, source_target_pairs={{0,4},{4,8},{8,12},{12,0},{1,5},{5,9},{9,13},{13,1},{2,6},{6,10},{... | collective-permute-start | bytes 2359304 | tf_op jit(solution)/shard_map/ppermute | solution.py:390
  120.4 23.4 %collective-permute-start.15 = (bf16[32,8192]{1,0:T(8,128)(2,1)}, bf16[32,8192]{1,0:T(8,128)(2,1)}, u32[]{:S(2)}, u32[]{:S(2)}) collective-permute-start(bf16[32,8192]{1,0:T(8,128)(2,1)} %slice.126), channel_id=1, source_target_pairs={{0,12},{4,0},{8,4},{12,8},{1,13},{5,1},{9,5},{13,9},{2,14},{6,2},{... | collective-permute-start | bytes 1572872 | tf_op jit(solution)/shard_map/ppermute | solution.py:395
  126.6 17.1 %collective-permute-start.14 = (bf16[16,8192]{1,0:T(8,128)(2,1)S(1)}, bf16[16,8192]{1,0:T(8,128)(2,1)S(1)}, u32[]{:S(2)}, u32[]{:S(2)}) collective-permute-start(bf16[16,8192]{1,0:T(8,128)(2,1)S(1)} %slice.125), channel_id=1, source_target_pairs={{0,4},{4,8},{8,12},{12,0},{1,5},{5,9},{9,13},{13,1},{2,6},{6,10},{... | collective-permute-start | bytes 786440 | tf_op jit(solution)/shard_map/ppermute | solution.py:394
  155.5 27.1 %collective-permute-start.18 = (bf16[576,1024]{1,0:T(8,128)(2,1)}, bf16[576,1024]{1,0:T(8,128)(2,1)}, u32[]{:S(2)}, u32[]{:S(2)}) collective-permute-start(bf16[576,1024]{1,0:T(8,128)(2,1)} %bitcast.21), channel_id=1, source_target_pairs={{0,1},{1,2},{2,3},{3,0},{4,5},{5,6},{6,7},{7,4},{8,9},{9,10},{10,1... | collective-permute-start | bytes 3538952 | tf_op jit(solution)/shard_map/ppermute | solution.py:401
  157.0 39.0 %collective-permute-start.19 = (bf16[576,1024]{1,0:T(8,128)(2,1)}, bf16[576,1024]{1,0:T(8,128)(2,1)}, u32[]{:S(2)}, u32[]{:S(2)}) collective-permute-start(bf16[576,1024]{1,0:T(8,128)(2,1)} %bitcast.22), channel_id=1, source_target_pairs={{0,3},{1,0},{2,1},{3,2},{4,7},{5,4},{6,5},{7,6},{8,11},{9,8},{10,9... | collective-permute-start | bytes 3538952 | tf_op jit(solution)/shard_map/ppermute | solution.py:401
  170.9 32.5 %collective-permute-start.23 = (bf16[64,4224]{1,0:T(8,128)(2,1)S(1)}, bf16[64,4224]{1,0:T(8,128)(2,1)S(1)}, u32[]{:S(2)}, u32[]{:S(2)}) collective-permute-start(bf16[64,4224]{1,0:T(8,128)(2,1)S(1)} %get-tuple-element.80), channel_id=1, source_target_pairs={{0,12},{4,0},{8,4},{12,8},{1,13},{5,1},{9,5},{13,9},{2,14},{6,2},{... | collective-permute-start | bytes 1622024 | tf_op jit(solution)/shard_map/ppermute | solution.py:401
  174.1 29.3 %collective-permute-start.22 = (bf16[80,4224]{1,0:T(8,128)(2,1)S(1)}, bf16[80,4224]{1,0:T(8,128)(2,1)S(1)}, u32[]{:S(2)}, u32[]{:S(2)}) collective-permute-start(bf16[80,4224]{1,0:T(8,128)(2,1)S(1)} %get-tuple-element.79), channel_id=1, source_target_pairs={{0,4},{4,8},{8,12},{12,0},{1,5},{5,9},{9,13},{13,1},{2,6},{6,10},{... | collective-permute-start | bytes 2027528 | tf_op jit(solution)/shard_map/ppermute | solution.py:401
  177.0 22.7 %collective-permute-start.16 = (bf16[16,4224]{1,0:T(8,128)(2,1)S(1)}, bf16[16,4224]{1,0:T(8,128)(2,1)S(1)}, u32[]{:S(2)}, u32[]{:S(2)}) collective-permute-start(bf16[16,4224]{1,0:T(8,128)(2,1)S(1)} %get-tuple-element.71), channel_id=1, source_target_pairs={{0,4},{4,8},{8,12},{12,0},{1,5},{5,9},{9,13},{13,1},{2,6},{6,10},{... | collective-permute-start | bytes 405512 | tf_op jit(solution)/shard_map/ppermute | solution.py:401
  182.6 17.1 %collective-permute-start.17 = (bf16[32,4224]{1,0:T(8,128)(2,1)S(1)}, bf16[32,4224]{1,0:T(8,128)(2,1)S(1)}, u32[]{:S(2)}, u32[]{:S(2)}) collective-permute-start(bf16[32,4224]{1,0:T(8,128)(2,1)S(1)} %get-tuple-element.72), channel_id=1, source_target_pairs={{0,12},{4,0},{8,4},{12,8},{1,13},{5,1},{9,5},{13,9},{2,14},{6,2},{... | collective-permute-start | bytes 811016 | tf_op jit(solution)/shard_map/ppermute | solution.py:401
  200.1 13.6 %collective-permute-start.20 = (bf16[48,4224]{1,0:T(8,128)(2,1)S(1)}, bf16[48,4224]{1,0:T(8,128)(2,1)S(1)}, u32[]{:S(2)}, u32[]{:S(2)}) collective-permute-start(bf16[48,4224]{1,0:T(8,128)(2,1)S(1)} %get-tuple-element.75), channel_id=1, source_target_pairs={{0,4},{4,8},{8,12},{12,0},{1,5},{5,9},{9,13},{13,1},{2,6},{6,10},{... | collective-permute-start | bytes 1216520 | tf_op jit(solution)/shard_map/ppermute | solution.py:406
  200.2 15.1 %collective-permute-start.21 = (bf16[48,4224]{1,0:T(8,128)(2,1)S(1)}, bf16[48,4224]{1,0:T(8,128)(2,1)S(1)}, u32[]{:S(2)}, u32[]{:S(2)}) collective-permute-start(bf16[48,4224]{1,0:T(8,128)(2,1)S(1)} %get-tuple-element.76), channel_id=1, source_target_pairs={{0,12},{4,0},{8,4},{12,8},{1,13},{5,1},{9,5},{13,9},{2,14},{6,2},{... | collective-permute-start | bytes 1216520 | tf_op jit(solution)/shard_map/ppermute | solution.py:406
  204.2 30.8 %collective-permute-start.24 = (bf16[144,4224]{1,0:T(8,128)(2,1)S(1)}, bf16[144,4224]{1,0:T(8,128)(2,1)S(1)}, u32[]{:S(2)}, u32[]{:S(2)}) collective-permute-start(bf16[144,4224]{1,0:T(8,128)(2,1)S(1)} %get-tuple-element.81), channel_id=1, source_target_pairs={{0,4},{4,8},{8,12},{12,0},{1,5},{5,9},{9,13},{13,1},{2,6},{6,10},{... | collective-permute-start | bytes 3649544 | tf_op jit(solution)/shard_map/ppermute | solution.py:406
  204.3 30.7 %collective-permute-start.25 = (bf16[144,4224]{1,0:T(8,128)(2,1)S(1)}, bf16[144,4224]{1,0:T(8,128)(2,1)S(1)}, u32[]{:S(2)}, u32[]{:S(2)}) collective-permute-start(bf16[144,4224]{1,0:T(8,128)(2,1)S(1)} %get-tuple-element.82), channel_id=1, source_target_pairs={{0,12},{4,0},{8,4},{12,8},{1,13},{5,1},{9,5},{13,9},{2,14},{6,2},{... | collective-permute-start | bytes 3649544 | tf_op jit(solution)/shard_map/ppermute | solution.py:406
  207.6 50.0 %collective-permute-start.30 = (bf16[1152,1024]{1,0:T(8,128)(2,1)S(1)}, bf16[1152,1024]{1,0:T(8,128)(2,1)S(1)}, u32[]{:S(2)}, u32[]{:S(2)}) collective-permute-start(bf16[1152,1024]{1,0:T(8,128)(2,1)S(1)} %get-tuple-element.74.refs_0_), channel_id=1, source_target_pairs={{0,1},{1,2},{2,3},{3,0},{4,5},{5,6},{6,7},{7,4},{8,9},{9,10},{10,1... | collective-permute-start | bytes 7077896 | tf_op jit(solution)/shard_map/ppermute | solution.py:406
  213.7 43.9 %collective-permute-start.31 = (bf16[1152,1024]{1,0:T(8,128)(2,1)S(1)}, bf16[1152,1024]{1,0:T(8,128)(2,1)S(1)}, u32[]{:S(2)}, u32[]{:S(2)}) collective-permute-start(bf16[1152,1024]{1,0:T(8,128)(2,1)S(1)} %get-tuple-element.83), channel_id=1, source_target_pairs={{0,3},{1,0},{2,1},{3,2},{4,7},{5,4},{6,5},{7,6},{8,11},{9,8},{10,9... | collective-permute-start | bytes 7077896 | tf_op jit(solution)/shard_map/ppermute | solution.py:406
  235.6 11.1 %collective-permute-start.26 = (bf16[48,4224]{1,0:T(8,128)(2,1)S(1)}, bf16[48,4224]{1,0:T(8,128)(2,1)S(1)}, u32[]{:S(2)}, u32[]{:S(2)}) collective-permute-start(bf16[48,4224]{1,0:T(8,128)(2,1)S(1)} %get-tuple-element.97), channel_id=1, source_target_pairs={{0,96},{16,112},{32,0},{48,16},{64,32},{80,48},{96,64},{112,80},{1... | collective-permute-start | bytes 1216520 | tf_op jit(solution)/shard_map/ppermute | solution.py:495
  236.5 16.0 %collective-permute-start.28 = (bf16[48,4224]{1,0:T(8,128)(2,1)S(1)}, bf16[48,4224]{1,0:T(8,128)(2,1)S(1)}, u32[]{:S(2)}, u32[]{:S(2)}) collective-permute-start(bf16[48,4224]{1,0:T(8,128)(2,1)S(1)} %get-tuple-element.95), channel_id=1, source_target_pairs={{0,32},{16,48},{32,64},{48,80},{64,96},{80,112},{96,0},{112,16},{1... | collective-permute-start | bytes 1216520 | tf_op jit(solution)/shard_map/ppermute | solution.py:495
  237.8 13.4 %collective-permute-start.27 = (bf16[48,4224]{1,0:T(8,128)(2,1)S(1)}, bf16[48,4224]{1,0:T(8,128)(2,1)S(1)}, u32[]{:S(2)}, u32[]{:S(2)}) collective-permute-start(bf16[48,4224]{1,0:T(8,128)(2,1)S(1)} %get-tuple-element.96), channel_id=1, source_target_pairs={{0,64},{16,80},{32,96},{48,112},{64,0},{80,16},{96,32},{112,48},{1... | collective-permute-start | bytes 1216520 | tf_op jit(solution)/shard_map/ppermute | solution.py:495
  252.6 8.1 %collective-permute-start.29 = (bf16[96,4224]{1,0:T(8,128)(2,1)S(1)}, bf16[96,4224]{1,0:T(8,128)(2,1)S(1)}, u32[]{:S(2)}, u32[]{:S(2)}) collective-permute-start(bf16[96,4224]{1,0:T(8,128)(2,1)S(1)} %pad_maximum_fusion), channel_id=1, source_target_pairs={{0,16},{16,0},{32,48},{48,32},{64,80},{80,64},{96,112},{112,96},{1... | collective-permute-start | bytes 2433032 | tf_op jit(solution)/shard_map/ppermute | solution.py:498
  (63 other events, 375.0 us)
where the time goes:
time: 265 us; the launch traced here: 264 us
  waiting for transfers between devices  116 us (44%)
  Pallas kernels  57.6 us (22%)
  starting transfers between devices  41.5 us (16%)
  local copies, waits for them, and re-layouts  39 us (15%)
  other arithmetic  6.06 us (2%)
    ppermute x3, waiting for transfers between devices, ring_gather(): right = lax.ppermute(block, axis, to_left)  34.2 us
    unnamed x126, local copies, waits for them, and re-layouts  31 us
    ppermute x3, waiting for transfers between devices, ring_second(): lax.ppermute(right, axis, to_right)  25.4 us
    pallas_call x3, Pallas kernels, forward(): pl.pallas_call(forward_kernel, grid=(steps,), in_specs=[pl.BlockSpec((p.s...  21.2 us
    ppermute x3, waiting for transfers between devices, body(): blocks[dz] = lax.ppermute(block, 'ep', shift(dz)) if dz else block  14.5 us
    pallas_call x2, Pallas kernels, weight_blocks(): pl.pallas_call(functools.partial(weight_kernel, len(xs), outs), grid_spec...  14.5 us
    ppermute x3, waiting for transfers between devices, body(): lax.ppermute(block, 'ep', shift(layers - dz))  14 us
    pallas_call x2, Pallas kernels, dx_blocks(): pl.pallas_call(functools.partial(dx_kernel, len(grads), bands), grid=(ste...  9.28 us
  transfers between devices with their start and end apart: 32, of which 16 were waited for; matrix products, arithmetic and copies ran while one was open for 3% of the time, Pallas kernels for 16%

commit v1 on v0

--- a/solution.py
+++ b/solution.py
@@ -22,6 +22,10 @@
 
 def cost(flops, size):
     return pl.CostEstimate(flops=int(flops), bytes_accessed=int(size), transcendentals=0)
+
+
+def in_hbm(*values):
+    return [pltpu.with_memory_space_constraint(v, pltpu.HBM) for v in values]
 
 
 def limit(mib):
@@ -81,9 +85,9 @@
     )(onehot, gate, inputs, upstream)
 
 
-def forward_kernel(*refs):
-    x_parts, dy_parts = refs[:5], refs[5:10]
-    gate_ref, up_ref, down_ref = refs[10:13]
+def forward_kernel(parts, *refs):
+    x_parts, dy_parts = refs[:parts], refs[parts : 2 * parts]
+    gate_ref, up_ref, down_ref = refs[2 * parts : 2 * parts + 3]
     x_ref, dy_ref, grads_ref, grads_t_ref, hidden_t_ref, prob_ref = refs[-9:-3]
     acc_g, acc_u, acc_b = refs[-3:]
     step = pl.program_id(0)
@@ -123,13 +127,16 @@
         hidden_t_ref[...] = hidden.T.astype(BF)
 
 
-def forward(parts, gate_w, up_w, down_w, after):
+def forward(parts, gate_w, up_w, down_w, after, pin, mib):
     width, part = gate_w.shape
     count = sum(p.shape[0] for p in parts)
     block = 1024
     steps = width // block
-    return pl.pallas_call(
-        forward_kernel,
+    pinned = (*parts, *parts, gate_w, up_w, down_w)
+    if pin:
+        pinned = in_hbm(*pinned)
+    return pl.pallas_call(
+        functools.partial(forward_kernel, len(parts)),
         grid=(steps,),
         in_specs=[pl.BlockSpec((p.shape[0], block), lambda i: (0, i)) for p in parts]
         + [pl.BlockSpec((p.shape[0], block), lambda i: (0, i + steps)) for p in parts]
@@ -148,55 +155,102 @@
             pl.BlockSpec((count, LANES), lambda i: (0, 0)),
         ],
         out_shape=[
-            jax.ShapeDtypeStruct((count, width), BF),
-            jax.ShapeDtypeStruct((count, width), BF),
-            jax.ShapeDtypeStruct((count, 2 * part), BF),
-            jax.ShapeDtypeStruct((2 * part, count), BF),
-            jax.ShapeDtypeStruct((part, count), BF),
-            jax.ShapeDtypeStruct((count, LANES), BF),
+            pltpu.HBM((count, width), BF),
+            pltpu.HBM((count, width), BF),
+            pltpu.HBM((count, 2 * part), BF),
+            pltpu.HBM((2 * part, count), BF),
+            pltpu.HBM((part, count), BF),
+            pltpu.HBM((count, LANES), BF),
         ],
         scratch_shapes=[pltpu.VMEM((count, part), F32)] * 3,
-        compiler_params=limit(30),
+        compiler_params=limit(mib),
         cost_estimate=cost(6 * count * width * part, 6 * width * part + 8 * count * width),
-    )(*parts, *parts, gate_w, up_w, down_w, *after)
-
-
-def weight_kernel(groups, outs, at_ref, *refs):
+    )(*pinned, *after)
+
+
+def weight_kernel(groups, own, at_ref, *refs):
     x_refs, dy_refs = refs[:groups], refs[groups : 2 * groups]
     g_refs, h_refs = refs[2 * groups : 3 * groups], refs[3 * groups : 4 * groups]
-    out_refs = refs[-outs:]
-    top = sum(dot(g[...], x[...]) for g, x in zip(g_refs, x_refs)).astype(BF)
-    low = sum(dot(h[...], d[...]) for h, d in zip(h_refs, dy_refs)).astype(BF)
-    if outs == 1:
-        out_refs[0][0, : top.shape[0], :] = top
-        out_refs[0][0, top.shape[0] :, :] = low
+    out_refs, (turned, tall_x, tall_dy) = refs[-5:-3], refs[-3:]
+    both = g_refs[0].shape[0]
+
+    @pl.when((pl.program_id(0) == 0) & (pl.program_id(1) == 0))
+    def _():
+        at = 0
+        for g, h in zip(g_refs, h_refs):
+            rows = g.shape[1]
+            turned[:both, at : at + rows] = g[...]
+            turned[both:, at : at + rows] = h[...]
+            at += rows
+
+    at = 0
+    for x, dy in zip(x_refs, dy_refs):
+        rows = x.shape[0]
+        tall_x[at : at + rows, :] = x[...]
+        tall_dy[at : at + rows, :] = dy[...]
+        at += rows
+    top = dot(turned[:both, :], tall_x[...]).astype(BF)
+    low = dot(turned[both:, :], tall_dy[...]).astype(BF)
+    if own:
+        sent = pl.program_id(0) < 2
+
+        @pl.when(sent)
+        def _():
+            out_refs[0][0, :both, :] = top
+            out_refs[0][0, both:, :] = low
+
+        @pl.when(jnp.logical_not(sent))
+        def _():
+            out_refs[1][:both, :] = top
+            out_refs[1][both:, :] = low
     else:
         half = out_refs[0].shape[1]
         out_refs[0][0] = top[:half]
-        out_refs[1][0, : top.shape[0] - half, :] = top[half:]
-        out_refs[1][0, top.shape[0] - half :, :] = low
-
-
-def weight_blocks(at, slice_w, xs, dys, grads_t, hiddens_t, outs, after=()):
-    block = 512
+        out_refs[1][0, : both - half, :] = top[half:]
+        out_refs[1][0, both - half :, :] = low
+
+
+def weight_blocks(at, slice_w, xs, dys, grads_t, hiddens_t, own, after=()):
+    block = 512 if own else 256
     steps = slice_w // block
     count = at.shape[0]
     rows = grads_t[0].shape[0] + hiddens_t[0].shape[0]
+    total = sum(v.shape[0] for v in xs)
     tall = [pl.BlockSpec((v.shape[0], block), lambda k, i, at: (0, at[k] * steps + i)) for v in xs]
-    whole = [pl.BlockSpec(v.shape, lambda k, i, at: (0, 0)) for v in list(grads_t) + list(hiddens_t)]
-    spec = pl.BlockSpec((1, rows // outs, block), lambda k, i, at: (k, 0, i))
-    return pl.pallas_call(
-        functools.partial(weight_kernel, len(xs), outs),
+    whole = [pl.BlockSpec(v.shape, lambda k, i, at: (0, 0)) for v in (*grads_t, *hiddens_t)]
+    if own:
+        last = steps - 1
+        out_specs = [
+            pl.BlockSpec(
+                (1, rows, block),
+                lambda k, i, at: (jnp.minimum(k, 1), 0, jnp.where(k < 2, i, last)),
+            ),
+            pl.BlockSpec((rows, block), lambda k, i, at: (0, jnp.where(k < 2, 0, i))),
+        ]
+        out_shape = [
+            jax.ShapeDtypeStruct((2, rows, slice_w), BF),
+            pltpu.HBM((rows, slice_w), BF),
+        ]
+    else:
+        out_specs = [pl.BlockSpec((1, rows // 2, block), lambda k, i, at: (k, 0, i))] * 2
+        out_shape = [jax.ShapeDtypeStruct((count, rows // 2, slice_w), BF)] * 2
+    return pl.pallas_call(
+        functools.partial(weight_kernel, len(xs), own),
         grid_spec=pltpu.PrefetchScalarGridSpec(
             num_scalar_prefetch=1,
             grid=(count, steps),
             in_specs=tall + tall + whole + [pl.BlockSpec(memory_space=pl.ANY)] * len(after),
-            out_specs=[spec] * outs,
+            out_specs=out_specs,
+            scratch_shapes=[
+                pltpu.VMEM((rows, total), BF),
+                pltpu.VMEM((total, block), BF),
+                pltpu.VMEM((total, block), BF),
+            ],
         ),
-        out_shape=[jax.ShapeDtypeStruct((count, rows // outs, slice_w), BF)] * outs,
+        out_shape=out_shape,
         compiler_params=limit(20),
-        cost_estimate=cost(count * 2 * rows * slice_w * sum(v.shape[0] for v in xs), count * 7 * MIB),
-    )(at, *xs, *dys, *grads_t, *hiddens_t, *after)
+        cost_estimate=cost(count * 2 * rows * slice_w * total, count * 7 * MIB),
+    )(at, *in_hbm(*xs, *dys, *grads_t, *hiddens_t), *after)
 
 
 def join_kernel(a_ref, b_ref, *refs):
@@ -220,6 +274,30 @@
     )(a, b, *after)
 
 
+def join_far_kernel(cut, near_l, near_r, pair_l, pair_r, far_l, far_r):
+    step = near_l.shape[0]
+    far_l[:cut, :] = near_l[:cut]
+    far_l[cut:, :] = pair_l[:step]
+    far_r[: step - cut, :] = near_r[cut:]
+    far_r[step - cut :, :] = pair_r[step:]
+
+
+def join_far(near_l, near_r, pair_l, pair_r, cut):
+    step, width = near_l.shape
+    block = 2048
+    parts = (near_l, near_r, pair_l, pair_r)
+    sizes = (cut + step, 2 * step - cut)
+    return pl.pallas_call(
+        functools.partial(join_far_kernel, cut),
+        grid=(width // block,),
+        in_specs=[pl.BlockSpec((p.shape[0], block), lambda i: (0, i)) for p in parts],
+        out_specs=[pl.BlockSpec((n, block), lambda i: (0, i)) for n in sizes],
+        out_shape=[jax.ShapeDtypeStruct((n, width), BF) for n in sizes],
+        compiler_params=limit(8),
+        cost_estimate=cost(0, 12 * step * width),
+    )(*parts)
+
+
 def pass_kernel(*refs):
     pass
 
@@ -240,7 +318,8 @@
     return (a.astype(F32) + b.astype(F32)).astype(BF)
 
 
-def dp_add_kernel(rest_ref, far_a_ref, far_b_ref, right_ref, left_ref):
+def dp_add_kernel(rest_ref, far_a_ref, far_b_ref, *refs):
+    right_ref, left_ref = refs[-2:]
     half = far_a_ref.shape[0]
     right_ref[:half, :] = add_rows(rest_ref[0, :half], far_a_ref[...])
     right_ref[half:, :] = rest_ref[0, half:]
@@ -248,7 +327,7 @@
     left_ref[half:, :] = add_rows(rest_ref[1, half:], far_b_ref[...])
 
 
-def dp_add(rest, far_a, far_b):
+def dp_add(rest, far_a, far_b, after):
     _, rows, width = rest.shape
     block = 256
     spec = pl.BlockSpec((rows // 2, block), lambda i: (0, i))
@@ -256,30 +335,32 @@
     return pl.pallas_call(
         dp_add_kernel,
         grid=(width // block,),
-        in_specs=[pl.BlockSpec((2, rows, block), lambda i: (0, 0, i)), spec, spec],
+        in_specs=[pl.BlockSpec((2, rows, block), lambda i: (0, 0, i)), spec, spec]
+        + [pl.BlockSpec(memory_space=pl.ANY)] * len(after),
         out_specs=[out, out],
         out_shape=[jax.ShapeDtypeStruct((rows, width), BF)] * 2,
         compiler_params=limit(12),
         cost_estimate=cost(2 * rows * width, 10 * rows * width),
-    )(rest, far_a, far_b)
-
-
-def etp_add_kernel(left_ref, right_ref, far_a_ref, far_b_ref, *refs):
+    )(rest, far_a, far_b, *after)
+
+
+def etp_add_kernel(to_left, to_right, left_ref, right_ref, far_a_ref, far_b_ref, *refs):
     left_out, right_out = refs[-2:]
-    cut = far_a_ref.shape[0]
-    right_out[:cut, :] = add_rows(right_ref[:cut], far_a_ref[...])
-    right_out[cut:, :] = right_ref[cut:]
-    left_out[:cut, :] = left_ref[:cut]
-    left_out[cut:, :] = add_rows(left_ref[cut:], far_b_ref[...])
-
-
-def etp_add(left, right, far_a, far_b, after):
+    right_out[...] = right_ref[...]
+    left_out[...] = left_ref[...]
+    for at, source, rows in to_right:
+        right_out[at : at + rows, :] = add_rows(right_ref[at : at + rows], far_a_ref[source : source + rows])
+    for at, source, rows in to_left:
+        left_out[at : at + rows, :] = add_rows(left_ref[at : at + rows], far_b_ref[source : source + rows])
+
+
+def etp_add(to_left, to_right, left, right, far_a, far_b, after):
     rows, width = left.shape
     block = 11 * LANES
     parts = (left, right, far_a, far_b)
     spec = pl.BlockSpec((rows, block), lambda i: (0, i))
     return pl.pallas_call(
-        etp_add_kernel,
+        functools.partial(etp_add_kernel, to_left, to_right),
         grid=(width // block,),
         in_specs=[pl.BlockSpec((p.shape[0], block), lambda i: (0, i)) for p in parts]
         + [pl.BlockSpec(memory_space=pl.ANY)] * len(after),
@@ -338,20 +419,21 @@
         out_specs=[pl.BlockSpec((rows, block), lambda i: (0, i)) for rows in sizes],
         out_shape=[jax.ShapeDtypeStruct((rows, width + LANES), BF) for rows in sizes],
         scratch_shapes=[pltpu.VMEM((count, 2 * part), BF), pltpu.VMEM((count, LANES), BF)],
-        compiler_params=limit(30),
+        compiler_params=limit(20),
         cost_estimate=cost(4 * count * width * part, 4 * width * part + 2 * count * width),
     )(*grads, *probs, gate_w, up_w, *after)
 
 
-def final_kernel(own_ref, left_ref, right_ref, gate_ref, up_ref, down_ref):
-    total = own_ref[0].astype(F32) + left_ref[...].astype(F32) + right_ref[...].astype(F32)
+def final_kernel(own_ref, left_ref, right_ref, *refs):
+    gate_ref, up_ref, down_ref = refs[-3:]
+    total = own_ref[...].astype(F32) + left_ref[...].astype(F32) + right_ref[...].astype(F32)
     part = down_ref.shape[0]
     gate_ref[...] = total[:part].T.astype(BF)
     up_ref[...] = total[part : 2 * part].T.astype(BF)
     down_ref[...] = total[2 * part :].astype(BF)
 
 
-def final_sum(rest, left, right):
+def final_sum(own, left, right, after):
     rows, width = left.shape
     part = rows // 3
     block = 256
@@ -360,40 +442,18 @@
     return pl.pallas_call(
         final_kernel,
         grid=(width // block,),
-        in_specs=[pl.BlockSpec((1, rows, block), lambda i: (2, 0, i)), spec, spec],
+        in_specs=[spec] * 3
+        + [pl.BlockSpec(memory_space=pl.ANY)] * len(after),
         out_specs=[tall, tall, pl.BlockSpec((part, block), lambda i: (0, i))],
         out_shape=[jax.ShapeDtypeStruct((width, part), BF)] * 2 + [jax.ShapeDtypeStruct((part, width), BF)],
         compiler_params=limit(16),
         cost_estimate=cost(rows * width, 8 * rows * width),
-    )(rest, left, right)
-
-
-def split_band(band, size):
-    first, second = [], []
-    for at, rows in band:
-        take = min(rows, size)
-        if take:
-            first.append((at, take))
-        if rows > take:
-            second.append((at + take, rows - take))
-        size -= take
-    return [first, second]
+    )(*in_hbm(own), left, right, *after)
 
 
 def ring(axis):
     size = lax.axis_size(axis)
     return [(i, (i + 1) % size) for i in range(size)], [(i, (i - 1) % size) for i in range(size)]
-
-
-def ring_gather(block, axis, cut, after=()):
-    to_right, to_left = ring(axis)
-    left = lax.ppermute(block, axis, to_right)
-    right = lax.ppermute(block, axis, to_left)
-    if after:
-        left, right = order(left, after), order(right, after)
-    far_a = lax.ppermute(left[:cut], axis, to_right)
-    far_b = lax.ppermute(right[cut:], axis, to_left)
-    return [block, left, right, far_a, far_b]
 
 
 def ring_first(far_a, far_b, axis):
@@ -435,60 +495,59 @@
         if dz == 2:
             block = order(block, (blocks[1],))
         blocks[dz] = lax.ppermute(block, "ep", shift(dz)) if dz else block
-    groups = [(0,), (1, 3), (2,)]
-    cuts = [32, 48, 16]
-    xs, dys, grads, grads_t, hiddens_t, probs = [], [], [], [], [], []
-    parts = [None] * len(groups)
-    for i, (group, cut) in enumerate(zip(groups, cuts)):
-        after = ()
-        if i == 1:
-            block = join_rows(blocks[group[0]], blocks[group[1]], tuple(parts[0][1:3]))
-        elif i == 2:
-            block = order(blocks[group[0]], tuple(parts[1][1:3] + parts[0][3:]))
-            after = (probs[0], *parts[1][3:])
-        else:
-            block = blocks[group[0]]
-        parts[i] = ring_gather(block, "etp", cut, after)
-        results = forward(parts[i], gate_w, up_w, down_w, probs[-1:])
-        for kept, result in zip((xs, dys, grads, grads_t, hiddens_t, probs), results):
-            kept.append(result)
+    step = 2 * CAP
+    weights = (gate_w, up_w, down_w)
+    to_right, to_left = ring("etp")
+    cut = 32
+    near = blocks[0]
+    near_l, near_r = lax.ppermute(near, "etp", to_right), lax.ppermute(near, "etp", to_left)
+    pair = join_rows(blocks[1], blocks[3], (near_l, near_r))
+    pair_l, pair_r = lax.ppermute(pair, "etp", to_right), lax.ppermute(pair, "etp", to_left)
+    far_l, far_r = join_far(near_l, near_r, pair_l, pair_r, cut)
+    far_l, far_r = lax.ppermute(far_l, "etp", to_right), lax.ppermute(far_r, "etp", to_left)
+    first = forward([near, near_l, near_r, pair, pair_l, pair_r], *weights, (), True, 28)
+
+    last = blocks[2]
+    last_l, last_r = lax.ppermute(last, "etp", to_right), lax.ppermute(last, "etp", to_left)
+    second = forward([last, last_l, last_r], *weights, first[-1:], True, 20)
+    last_l, last_r = order(last_l, second[-1:]), order(last_r, second[-1:])
+    last_fl = lax.ppermute(last_l[: step - cut], "etp", to_right)
+    last_fr = lax.ppermute(last_r[step - cut :], "etp", to_left)
+    bands = [[(k * step, step), ((3 + 2 * k) * step, 2 * step)] for k in range(3)]
+    bands += [[((9 + k) * step, step)] for k in range(3)]
+    sources = [first[2], second[2]], [first[5], second[5]]
+    own_p, left_p, right_p, own_q, left_q, right_q = dx_blocks(*sources, gate_w, up_w, bands, ())
+    third = forward([far_l, far_r, last_fl, last_fr], *weights, (own_p,), False, 16)
+    xs, dys, _, grads_t, hiddens_t, _ = zip(first, second, third)
 
     dp = lax.axis_size("dp")
     slice_w = width // dp
     my_dp = lax.axis_index("dp")
 
-    def weights_for(ahead, outs, after=()):
+    def weights_for(ahead, own, after=()):
         at = jnp.stack([(my_dp + k) % dp for k in ahead]).astype(jnp.int32)
-        return weight_blocks(at, slice_w, xs, dys, grads_t, hiddens_t, outs, after)
-
-    far_a, far_b = weights_for((2,), 2)
+        return weight_blocks(at, slice_w, xs, dys, grads_t, hiddens_t, own, after)
+
+    far_a, far_b = weights_for((2,), False)
     got_wa, got_wb = ring_first(far_a[0], far_b[0], "dp")
-
-    step = 2 * CAP
-    plans = [
-        ((1, 2), (1, 3, 2), [(0, 2 * step), (8 * step, step)], 80, 64),
-        ((0,), (0,), [(0, step)], 16, 32),
-    ]
-    pieces, got = [], []
-    after = (far_a,)
-    for sources, members, firsts, size_a, size_b in plans:
-        bands = [[(at + k * rows, rows) for at, rows in firsts] for k in range(3)]
-        far = [(at + 3 * rows, rows) for at, rows in firsts]
-        bands += split_band(far, size_a)
-        out = dx_blocks([grads[k] for k in sources], [probs[k] for k in sources], gate_w, up_w, bands, after)
-        pieces.append(out)
-        got.append(ring_first(out[3], out[4], "etp"))
-        after = (out[0],)
-
-    (rest,) = weights_for((1, dp - 1, 0), 1, after)
-    right_w, left_w = dp_add(rest, got_wa, got_wb)
+    wide = cut + step
+    more = 3 * step - wide
+    bands = [[(0, wide), (3 * step, step - cut)], [(wide, more), (4 * step - cut, cut)]]
+    far_l, far_r = dx_blocks([third[2]], [third[5]], gate_w, up_w, bands, (far_a,))
+    got_l, got_r = ring_first(far_l, far_r, "etp")
+
+    rest, own_w = weights_for((1, dp - 1, 0), True, (far_l,))
+    plan_p = [(cut, 0, step - cut), (2 * step, step - cut, step)], [(0, 0, cut), (step, cut, step)]
+    plan_q = [(step - cut, more, cut)], [(0, wide, step - cut)]
+    left_q, right_q = etp_add(*plan_q, left_q, right_q, got_l, got_r, (rest,))
+    left_p, right_p = etp_add(*plan_p, left_p, right_p, got_l, got_r, (rest,))
+    right_w, left_w = dp_add(rest, got_wa, got_wb, (left_q, left_p))
     from_left_w, from_right_w = ring_second(left_w, right_w, "dp")
 
     returned = {}
-    for (sources, members, *_), out, far in zip(plans, pieces, got):
-        own, left, right = out[:3]
-        left, right = etp_add(left, right, *far, (right_w,))
+    for members, own, left, right in [((2,), own_q, left_q, right_q), ((0, 1, 3), own_p, left_p, right_p)]:
         from_left, from_right = ring_second(left, right, "etp")
+        from_left = order(from_left, (right_w,))
         total = (own.astype(F32) + from_left.astype(F32) + from_right.astype(F32)).astype(BF)
         for i, dz in enumerate(members):
             block = total[i * step : (i + 1) * step]
@@ -504,7 +563,7 @@
     per_expert = jnp.sum(jnp.where(onehot, prob_slots[:, :, None], 0.0), axis=1)
     grad_probs = jnp.sum(jnp.where(chosen, per_expert.T[:, None, :], 0.0), axis=2)
 
-    grad_gate, grad_up, grad_down = final_sum(rest, from_left_w, from_right_w)
+    grad_gate, grad_up, grad_down = final_sum(own_w, from_left_w, from_right_w, (grad_inputs,))
     return (grad_inputs, grad_probs, grad_gate[None], grad_up[None], grad_down[None])
 
 

time: 265 us -> 240 us (0.906)
  waiting for transfers between devices: 116 us -> 93.6 us
  local copies, waits for them, and re-layouts: 39 us -> 17.4 us
  Pallas kernels: 57.6 us -> 78.9 us
  starting transfers between devices: 41.5 us -> 36.3 us
  other arithmetic: 6.06 us -> 9.11 us
    ppermute x12 -> x10, waiting for transfers between devices: 48.8 us -> 21 us  [the longest x1 13 us: body(): lax.ppermute(pair, 'etp', to_left)]
    pallas_call x8 -> x9, Pallas kernels: 40 us -> 61.2 us  [the longest x3 29 us: forward(): pl.pallas_call(functools.partial(forward_kernel, len(parts)), grid=(steps...]
    ppermute x3, waiting for transfers between devices: 14.5 us -> 32.2 us  [body(): blocks[dz] = lax.ppermute(block, 'ep', shift(dz)) if dz else block]
    unnamed x126 -> x86, local copies, waits for them, and re-layouts: 31 us -> 13.4 us
    ppermute x3, waiting for transfers between devices: 14 us -> 7.45 us  [body(): lax.ppermute(block, 'ep', shift(layers - dz))]
    ppermute x3, waiting for transfers between devices: 25.4 us -> 19 us  [ring_second(): lax.ppermute(right, axis, to_right)]
    ppermute x3 -> x2, starting transfers between devices: 7.81 us -> 2.51 us  [ring_first(): lax.ppermute(far_b, axis, to_left)]
    ppermute x3 -> x2, waiting for transfers between devices: 5.48 us -> 1.22 us  [ring_first(): lax.ppermute(far_a, axis, to_right)]
  transfers between devices with their start and end apart: 32 -> 28, of which waited for: 16 -> 16; matrix products, arithmetic and copies ran while one was open for 3% -> 5% of each run, Pallas kernels for 16% -> 23%
where the time goes in v1:
time: 240 us; the launch traced here: 239 us
  waiting for transfers between devices  93.6 us (39%)
  Pallas kernels  78.9 us (33%)
  starting transfers between devices  36.3 us (15%)
  local copies, waits for them, and re-layouts  17.4 us (7%)
  other arithmetic  9.11 us (4%)
    ppermute x3, waiting for transfers between devices, body(): blocks[dz] = lax.ppermute(block, 'ep', shift(dz)) if dz else block  32.2 us
    pallas_call x3, Pallas kernels, forward(): pl.pallas_call(functools.partial(forward_kernel, len(parts)), grid=(steps...  29 us
    pallas_call x2, Pallas kernels, weight_blocks(): pl.pallas_call(functools.partial(weight_kernel, len(xs), own), grid_spec=...  19.5 us
    ppermute x3, waiting for transfers between devices, ring_second(): lax.ppermute(right, axis, to_right)  19 us
    unnamed x86, local copies, waits for them, and re-layouts  13.4 us
    ppermute x1, waiting for transfers between devices, body(): lax.ppermute(pair, 'etp', to_left)  13 us
    pallas_call x2, Pallas kernels, dx_blocks(): pl.pallas_call(functools.partial(dx_kernel, len(grads), bands), grid=(ste...  9.93 us
    ppermute x3, starting transfers between devices, ring_second(): lax.ppermute(left, axis, to_left)  7.6 us
  transfers between devices with their start and end apart: 28, of which 16 were waited for; matrix products, arithmetic and copies ran while one was open for 5% of the time, Pallas kernels for 23%

profile of v1, /device:TPU:0, one launch (start us, length us, event | category | flops | bytes accessed | tf_op | source)
XLA Modules:
  0.0 238.8 jit_solution(15614554836379366896)
XLA Ops:
  7.6 2.9 %shard_map.110 = (bf16[96,8192]{1,0:T(8,128)(2,1)S(1)}, bf16[96,8192]{1,0:T(8,128)(2,1)S(1)}) custom-call(bf16[192,256]{1,0:T(8,128)(2,1)S(1)} %get-tuple-element.109.onehot_ref, f32[192,1]{1,0:T(8,128)S(1)} %reshape.77.gate_ref, bf16[256,4096]{1,0:T(8,128)(2,1)S(1)} %copy-done.14, bf16[256,4096]{1,0:T(8,128)(2,1)S(1)} %copy-done.15), custom_call_target="tpu_custom_call" | custom-call | flops 805306368 | bytes 8388608 | tf_op jit(solution)/shard_map/pallas_call | solution.py:72
  10.7 3.3 %collective-permute-done = bf16[96,8192]{1,0:T(8,128)(2,1)S(1)} collective-permute-done((bf16[96,8192]{1,0:T(8,128)(2,1)S(1)}, bf16[96,8192]{1,0:T(8,128)(2,1)S(1)}, u32[]{:S(2)}, u32[]{:S(2)}) %collective-permute-start) | collective-permute-done | bytes 1572896 | tf_op jit(solution)/shard_map/ppermute | solution.py:488
  16.3 2.2 collective-permute-start.4
  18.6 3.1 %collective-permute-start.2 = (bf16[48,8192]{1,0:T(8,128)(2,1)S(1)}, bf16[48,8192]{1,0:T(8,128)(2,1)S(1)}, u32[]{:S(2)}, u32[]{:S(2)}) collective-permute-start(bf16[48,8192]{1,0:T(8,128)(2,1)S(1)} %pad_maximum_fusion.1.refs_0_.refs_6_), channel_id=1, source_target_pairs={{0,12},{4,0},{8,4},{12,8},{1,13},{5,1},{9,5},{13,9},{2,14},{6,2},{... | collective-permute-start | bytes 2359304 | tf_op jit(solution)/shard_map/ppermute | solution.py:503
  21.7 14.5 %collective-permute-done.3.a_ref.refs_1_ = bf16[48,8192]{1,0:T(8,128)(2,1)S(1)} collective-permute-done((bf16[48,8192]{1,0:T(8,128)(2,1)S(1)}, bf16[48,8192]{1,0:T(8,128)(2,1)S(1)}, u32[]{:S(2)}, u32[]{:S(2)}) %collective-permute-start.3) | collective-permute-done | bytes 786464 | tf_op jit(solution)/shard_map/ppermute | solution.py:497
  36.2 2.3 collective-permute-done.2.refs_1_.refs_2_.refs_8_.near_r
  38.5 3.4 %collective-permute-done.1.refs_0_.refs_1_.refs_7_.near_l = bf16[48,8192]{1,0:T(8,128)(2,1)S(1)} collective-permute-done((bf16[48,8192]{1,0:T(8,128)(2,1)S(1)}, bf16[48,8192]{1,0:T(8,128)(2,1)S(1)}, u32[]{:S(2)}, u32[]{:S(2)}) %collective-permute-start.1) | collective-permute-done | bytes 786464 | tf_op jit(solution)/shard_map/ppermute | solution.py:503
  47.4 17.7 %collective-permute-done.7.refs_0_.refs_3_ = bf16[48,8192]{1,0:T(8,128)(2,1)S(1)} collective-permute-done((bf16[48,8192]{1,0:T(8,128)(2,1)}, bf16[48,8192]{1,0:T(8,128)(2,1)S(1)}, u32[]{:S(2)}, u32[]{:S(2)}) %collective-permute-start.7) | collective-permute-done | bytes 786464 | tf_op jit(solution)/shard_map/ppermute | solution.py:497
  65.1 2.1 collective-permute-start.9
  67.1 13.0 %collective-permute-done.6.refs_5_.refs_11_.pair_r = bf16[96,8192]{1,0:T(8,128)(2,1)S(1)} collective-permute-done((bf16[96,8192]{1,0:T(8,128)(2,1)S(1)}, bf16[96,8192]{1,0:T(8,128)(2,1)S(1)}, u32[]{:S(2)}, u32[]{:S(2)}) %collective-permute-start.6) | collective-permute-done | bytes 1572896 | tf_op jit(solution)/shard_map/ppermute | solution.py:505
  84.2 3.9 %shard_map.116 = (bf16[80,8192]{1,0:T(8,128)(2,1)}, bf16[64,8192]{1,0:T(8,128)(2,1)}) custom-call(bf16[48,8192]{1,0:T(8,128)(2,1)S(1)} %copy-done.9, bf16[48,8192]{1,0:T(8,128)(2,1)S(1)} %copy-done.7, bf16[96,8192]{1,0:T(8,128)(2,1)} %collective-permute-done.5.refs_4_.refs_10_.pair_l, bf16[96,8192]{1,0:T(8,128)(2,1)S(1)} %collective-permute-done.6.refs_5_.refs_11_.pair_r), custom_call_target="tpu_custom_call" | custom-call | bytes 4718592 | tf_op jit(solution)/shard_map/pallas_call | solution.py:290
  88.5 3.0 %collective-permute-start.11 = (bf16[64,8192]{1,0:T(8,128)(2,1)}, bf16[64,8192]{1,0:T(8,128)(2,1)}, u32[]{:S(2)}, u32[]{:S(2)}) collective-permute-start(bf16[64,8192]{1,0:T(8,128)(2,1)} %get-tuple-element.58), channel_id=1, source_target_pairs={{0,12},{4,0},{8,4},{12,8},{1,13},{5,1},{9,5},{13,9},{2,14},{6,2},{... | collective-permute-start | bytes 3145736 | tf_op jit(solution)/shard_map/ppermute | solution.py:507
  91.4 13.4 %shard_map.112 = (bf16[432,4096]{1,0:T(8,128)(2,1)}, bf16[432,4096]{1,0:T(8,128)(2,1)}, bf16[432,768]{1,0:T(8,128)(2,1)}, bf16[768,432]{1,0:T(8,128)(2,1)}, bf16...) custom-call(bf16[48,8192]{1,0:T(8,128)(2,1)} %copy-done.35, bf16[48,8192]{1,0:T(8,128)(2,1)} %copy-done.8, ...), custom_call_target="tpu_custom_call" | custom-call | flops 4076863488 | bytes 23592960 | tf_op jit(solution)/shard_map/pallas_call | solution.py:138
  106.9 8.0 %shard_map.114 = (bf16[144,4096]{1,0:T(8,128)(2,1)}, bf16[144,4096]{1,0:T(8,128)(2,1)}, bf16[144,768]{1,0:T(8,128)(2,1)}, bf16[768,144]{1,0:T(8,128)(2,1)}, bf16...) custom-call(bf16[48,8192]{1,0:T(8,128)(2,1)} %copy-done.36, bf16[48,8192]{1,0:T(8,128)(2,1)} %copy-done.34, ...), custom_call_target="tpu_custom_call" | custom-call | flops 1358954496 | bytes 14155776 | tf_op jit(solution)/shard_map/pallas_call | solution.py:138
  117.9 2.3 collective-permute-start.12
  123.2 6.3 %shard_map.115 = (bf16[144,4224]{1,0:T(8,128)(2,1)S(1)}, bf16[144,4224]{1,0:T(8,128)(2,1)S(1)}, bf16[144,4224]{1,0:T(8,128)(2,1)S(1)}, bf16[48,4224]{1,0:T(8,128...) custom-call(bf16[432,768]{1,0:T(8,128)(2,1)S(1)} %copy-done.31, bf16[144,768]{1,0:T(8,128)(2,1)S(1)} %copy-done.32, ...), custom_call_target="tpu_custom_call" | custom-call | flops 3623878656 | bytes 11010048 | tf_op jit(solution)/shard_map/pallas_call | solution.py:413
  130.1 7.6 %shard_map.119 = (bf16[192,4096]{1,0:T(8,128)(2,1)}, bf16[192,4096]{1,0:T(8,128)(2,1)}, bf16[192,768]{1,0:T(8,128)(2,1)}, bf16[768,192]{1,0:T(8,128)(2,1)}, bf16...) custom-call(bf16[80,8192]{1,0:T(8,128)(2,1)} %collective-permute-done.10.refs_0_.refs_4_, ...), custom_call_target="tpu_custom_call" | custom-call | flops 1811939328 | bytes 15728640 | tf_op jit(solution)/shard_map/pallas_call | solution.py:138
  137.8 6.7 %shard_map.120 = (bf16[1,576,1024]{2,1,0:T(8,128)(2,1)}, bf16[1,576,1024]{2,1,0:T(8,128)(2,1)}) custom-call(s32[1]{0:T(128)} %bitcast.17.at_ref, bf16[432,4096]{1,0:T(8,128)(2,1)} %get-tuple-element.61.refs_0_, bf16[144,4096]{1,0:T(8,128)(2,1)} %get-tuple-element.62.refs_1_, bf16[192,4096]{1,0:T(8,128)(2,1)} %get-tuple-element.63.refs_2_, ...), custom_call_target="tpu_custom_call" | custom-call | flops 1811939328 | bytes 7340032 | tf_op jit(solution)/shard_map/pallas_call | solution.py:237
  146.1 3.6 %shard_map.121 = (bf16[96,4224]{1,0:T(8,128)(2,1)}, bf16[96,4224]{1,0:T(8,128)(2,1)}) custom-call(bf16[192,768]{1,0:T(8,128)(2,1)S(1)} %copy-done.26, bf16[192,128]{1,0:T(8,128)(2,1)S(1)} %copy-done.30, bf16[4096,384]{1,0:T(8,128)(2,1)S(1)} %bitcast.43, bf16[4096,384]{1,0:T(8,128)(2,1)S(1)} %bitcast.48, bf16[1,576,1024]{2,1,0:T(8,128)(2,1)} %get-tuple-element.73.refs_4_), custom_call_target="tpu_custom_call" | custom-call | flops 1207959552 | bytes 7864320 | tf_op jit(solution)/shard_map/pallas_call | solution.py:413
  153.6 12.7 %shard_map.122 = (bf16[2,1152,1024]{2,1,0:T(8,128)(2,1)S(1)}, bf16[1152,1024]{1,0:T(8,128)(2,1)}) custom-call(s32[3]{0:T(128)S(1)} %pad_add_fusion.at_ref, bf16[432,4096]{1,0:T(8,128)(2,1)} %get-tuple-element.61.refs_0_, bf16[144,4096]{1,0:T(8,128)(2,1)} %get-tuple-element.62.refs_1_, bf16[192,4096]{1,0:T(8,128)(2,1)} %get-tuple-element.63.refs_2_, ...), custom_call_target="tpu_custom_call" | custom-call | flops 5435817984 | bytes 22020096 | tf_op jit(solution)/shard_map/pallas_call | solution.py:237
  170.1 2.6 %collective-permute-start.22 = (bf16[48,4224]{1,0:T(8,128)(2,1)}, bf16[48,4224]{1,0:T(8,128)(2,1)}, u32[]{:S(2)}, u32[]{:S(2)}) collective-permute-start(bf16[48,4224]{1,0:T(8,128)(2,1)} %get-tuple-element.81.refs_0_), channel_id=1, source_target_pairs={{0,12},{4,0},{8,4},{12,8},{1,13},{5,1},{9,5},{13,9},{2,14},{6,2},{... | collective-permute-start | bytes 1216520 | tf_op jit(solution)/shard_map/ppermute | solution.py:466
  172.7 2.2 shard_map.123
  174.9 3.2 %collective-permute-start.19 = (bf16[144,4224]{1,0:T(8,128)(2,1)}, bf16[144,4224]{1,0:T(8,128)(2,1)}, u32[]{:S(2)}, u32[]{:S(2)}) collective-permute-start(bf16[144,4224]{1,0:T(8,128)(2,1)} %get-tuple-element.82.refs_1_), channel_id=1, source_target_pairs={{0,12},{4,0},{8,4},{12,8},{1,13},{5,1},{9,5},{13,9},{2,14},{6,2},{... | collective-permute-start | bytes 3649544 | tf_op jit(solution)/shard_map/ppermute | solution.py:466
  178.1 4.4 %shard_map.125 = (bf16[1152,1024]{1,0:T(8,128)(2,1)S(1)}, bf16[1152,1024]{1,0:T(8,128)(2,1)}) custom-call(bf16[2,1152,1024]{2,1,0:T(8,128)(2,1)S(1)} %get-tuple-element.76.refs_0_.rest_ref, bf16[576,1024]{1,0:T(8,128)(2,1)} %collective-permute-done.17.far_a_ref, bf16[576,1024]{1,0:T(8,128)(2,1)S(1)} %collective-permute-done.18.far_b_ref, ...), custom_call_target="tpu_custom_call" | custom-call | flops 2359296 | bytes 11796480 | tf_op jit(solution)/shard_map/pallas_call | solution.py:335
  188.6 15.5 %collective-permute-done.16.refs_0_ = bf16[144,4224]{1,0:T(8,128)(2,1)} collective-permute-done((bf16[144,4224]{1,0:T(8,128)(2,1)}, bf16[144,4224]{1,0:T(8,128)(2,1)}, u32[]{:S(2)}, u32[]{:S(2)}) %collective-permute-start.16) | collective-permute-done | bytes 1216544 | tf_op jit(solution)/shard_map/ppermute | solution.py:466
  204.1 2.5 %add_convert_fusion = bf16[144,4224]{1,0:T(8,128)(2,1)S(1)} fusion(bf16[144,4224]{1,0:T(8,128)(2,1)} %collective-permute-done.19, bf16[144,4224]{1,0:T(8,128)(2,1)} %shard_map.126, bf16[144,4224]{1,0:T(8,128)(2,1)} %copy-done.12), kind=kLoop, calls=%fused_computation.1 | loop fusion | flops 3649536 | bytes 4866048 | tf_op jit(solution)/shard_map/convert_element_type | solution.py:551
  208.8 5.8 %collective-permute-done.20 = bf16[48,4224]{1,0:T(8,128)(2,1)S(1)} collective-permute-done((bf16[48,4224]{1,0:T(8,128)(2,1)S(1)}, bf16[48,4224]{1,0:T(8,128)(2,1)S(1)}, u32[]{:S(2)}, u32[]{:S(2)}) %collective-permute-start.20) | collective-permute-done | bytes 405536 | tf_op jit(solution)/shard_map/ppermute | solution.py:554
  216.5 2.3 collective-permute-done.25
  221.2 2.2 convolution_convert_fusion.refs_0_
  223.3 6.7 %collective-permute-done.27.right_ref = bf16[1152,1024]{1,0:T(8,128)(2,1)} collective-permute-done((bf16[1152,1024]{1,0:T(8,128)(2,1)}, bf16[1152,1024]{1,0:T(8,128)(2,1)}, u32[]{:S(2)}, u32[]{:S(2)}) %collective-permute-start.27) | collective-permute-done | bytes 2359328 | tf_op jit(solution)/shard_map/ppermute | solution.py:466
  230.1 3.5 %collective-permute-done.26.left_ref = bf16[1152,1024]{1,0:T(8,128)(2,1)} collective-permute-done((bf16[1152,1024]{1,0:T(8,128)(2,1)S(1)}, bf16[1152,1024]{1,0:T(8,128)(2,1)}, u32[]{:S(2)}, u32[]{:S(2)}) %collective-permute-start.26) | collective-permute-done | bytes 2359328 | tf_op jit(solution)/shard_map/ppermute | solution.py:466
  233.6 5.1 %shard_map.128 = (bf16[1024,384]{1,0:T(8,128)(2,1)}, bf16[1024,384]{1,0:T(8,128)(2,1)}, bf16[384,1024]{1,0:T(8,128)(2,1)}) custom-call(bf16[1152,1024]{1,0:T(8,128)(2,1)} %get-tuple-element.86.own_ref, bf16[1152,1024]{1,0:T(8,128)(2,1)} %collective-permute-done.26.left_ref, bf16[1152,1024]{1,0:T(8,128)(2,1)} %collective-permute-done.27.right_ref, ...), custom_call_target="tpu_custom_call" | custom-call | flops 1179648 | bytes 9437184 | tf_op jit(solution)/shard_map/pallas_call | solution.py:442
  (167 shorter events, 49.6 us)
Async XLA Ops:
  10.5 3.5 %collective-permute-start = (bf16[96,8192]{1,0:T(8,128)(2,1)S(1)}, bf16[96,8192]{1,0:T(8,128)(2,1)S(1)}, u32[]{:S(2)}, u32[]{:S(2)}) collective-permute-start(bf16[96,8192]{1,0:T(8,128)(2,1)S(1)} %get-tuple-element.49), channel_id=1, source_target_pairs={{0,16},{16,0},{32,48},{48,32},{64,80},{80,64},{96,112},{112,96},{1... | collective-permute-start | bytes 4718600 | tf_op jit(solution)/shard_map/ppermute | solution.py:488
  14.2 22.0 %collective-permute-start.3 = (bf16[48,8192]{1,0:T(8,128)(2,1)S(1)}, bf16[48,8192]{1,0:T(8,128)(2,1)S(1)}, u32[]{:S(2)}, u32[]{:S(2)}) collective-permute-start(bf16[48,8192]{1,0:T(8,128)(2,1)S(1)} %pad_maximum_fusion.2), channel_id=1, source_target_pairs={{0,32},{16,48},{32,64},{48,80},{64,96},{80,112},{96,0},{112,16},{1... | collective-permute-start | bytes 2359304 | tf_op jit(solution)/shard_map/ppermute | solution.py:497
  16.3 19.9 %collective-permute-start.4 = (bf16[48,8192]{1,0:T(8,128)(2,1)S(1)}, bf16[48,8192]{1,0:T(8,128)(2,1)S(1)}, u32[]{:S(2)}, u32[]{:S(2)}) collective-permute-start(bf16[48,8192]{1,0:T(8,128)(2,1)S(1)} %pad_maximum_fusion.3), channel_id=1, source_target_pairs={{0,96},{16,112},{32,0},{48,16},{64,32},{80,48},{96,64},{112,80},{1... | collective-permute-start | bytes 2359304 | tf_op jit(solution)/shard_map/ppermute | solution.py:497
  18.6 23.8 %copy-start.35 = (bf16[48,8192]{1,0:T(8,128)(2,1)}, bf16[48,8192]{1,0:T(8,128)(2,1)S(1)}, u32[]{:S(2)}) copy-start(bf16[48,8192]{1,0:T(8,128)(2,1)S(1)} %pad_maximum_fusion.1.refs_0_.refs_6_) | copy-start | bytes 2359300
  18.6 19.9 %collective-permute-start.2 = (bf16[48,8192]{1,0:T(8,128)(2,1)S(1)}, bf16[48,8192]{1,0:T(8,128)(2,1)S(1)}, u32[]{:S(2)}, u32[]{:S(2)}) collective-permute-start(bf16[48,8192]{1,0:T(8,128)(2,1)S(1)} %pad_maximum_fusion.1.refs_0_.refs_6_), channel_id=1, source_target_pairs={{0,12},{4,0},{8,4},{12,8},{1,13},{5,1},{9,5},{13,9},{2,14},{6,2},{... | collective-permute-start | bytes 2359304 | tf_op jit(solution)/shard_map/ppermute | solution.py:503
  21.7 20.2 %collective-permute-start.1 = (bf16[48,8192]{1,0:T(8,128)(2,1)S(1)}, bf16[48,8192]{1,0:T(8,128)(2,1)S(1)}, u32[]{:S(2)}, u32[]{:S(2)}) collective-permute-start(bf16[48,8192]{1,0:T(8,128)(2,1)S(1)} %pad_maximum_fusion.1.refs_0_.refs_6_), channel_id=1, source_target_pairs={{0,4},{4,8},{8,12},{12,0},{1,5},{5,9},{9,13},{13,1},{2,6},{6,10},{... | collective-permute-start | bytes 2359304 | tf_op jit(solution)/shard_map/ppermute | solution.py:503
  42.8 37.3 %collective-permute-start.6 = (bf16[96,8192]{1,0:T(8,128)(2,1)S(1)}, bf16[96,8192]{1,0:T(8,128)(2,1)S(1)}, u32[]{:S(2)}, u32[]{:S(2)}) collective-permute-start(bf16[96,8192]{1,0:T(8,128)(2,1)S(1)} %shard_map.111.refs_3_.refs_9_), channel_id=1, source_target_pairs={{0,12},{4,0},{8,4},{12,8},{1,13},{5,1},{9,5},{13,9},{2,14},{6,2},{... | collective-permute-start | bytes 4718600 | tf_op jit(solution)/shard_map/ppermute | solution.py:505
  43.3 38.6 %collective-permute-start.5 = (bf16[96,8192]{1,0:T(8,128)(2,1)S(1)}, bf16[96,8192]{1,0:T(8,128)(2,1)}, u32[]{:S(2)}, u32[]{:S(2)}) collective-permute-start(bf16[96,8192]{1,0:T(8,128)(2,1)S(1)} %shard_map.111.refs_3_.refs_9_), channel_id=1, source_target_pairs={{0,4},{4,8},{8,12},{12,0},{1,5},{5,9},{9,13},{13,1},{2,6},{6,10},{... | collective-permute-start | bytes 4718600 | tf_op jit(solution)/shard_map/ppermute | solution.py:505
  45.8 19.3 %collective-permute-start.7 = (bf16[48,8192]{1,0:T(8,128)(2,1)}, bf16[48,8192]{1,0:T(8,128)(2,1)S(1)}, u32[]{:S(2)}, u32[]{:S(2)}) collective-permute-start(bf16[48,8192]{1,0:T(8,128)(2,1)} %shard_map.113), channel_id=1, source_target_pairs={{0,64},{16,80},{32,96},{48,112},{64,0},{80,16},{96,32},{112,48},{1... | collective-permute-start | bytes 2359304 | tf_op jit(solution)/shard_map/ppermute | solution.py:497
  65.1 23.1 %copy-start.36 = (bf16[48,8192]{1,0:T(8,128)(2,1)}, bf16[48,8192]{1,0:T(8,128)(2,1)S(1)}, u32[]{:S(2)}) copy-start(bf16[48,8192]{1,0:T(8,128)(2,1)S(1)} %collective-permute-done.7.refs_0_.refs_3_) | copy-start | bytes 2359300
  65.1 39.8 %collective-permute-start.9 = (bf16[48,8192]{1,0:T(8,128)(2,1)S(1)}, bf16[48,8192]{1,0:T(8,128)(2,1)S(1)}, u32[]{:S(2)}, u32[]{:S(2)}) collective-permute-start(bf16[48,8192]{1,0:T(8,128)(2,1)S(1)} %collective-permute-done.7.refs_0_.refs_3_), channel_id=1, source_target_pairs={{0,12},{4,0},{8,4},{12,8},{1,13},{5,1},{9,5},{13,9},{2,14},{6,2},{... | collective-permute-start | bytes 2359304 | tf_op jit(solution)/shard_map/ppermute | solution.py:511
  67.1 37.7 %collective-permute-start.8 = (bf16[48,8192]{1,0:T(8,128)(2,1)S(1)}, bf16[48,8192]{1,0:T(8,128)(2,1)S(1)}, u32[]{:S(2)}, u32[]{:S(2)}) collective-permute-start(bf16[48,8192]{1,0:T(8,128)(2,1)S(1)} %collective-permute-done.7.refs_0_.refs_3_), channel_id=1, source_target_pairs={{0,4},{4,8},{8,12},{12,0},{1,5},{5,9},{9,13},{13,1},{2,6},{6,10},{... | collective-permute-start | bytes 2359304 | tf_op jit(solution)/shard_map/ppermute | solution.py:511
  88.1 42.0 %collective-permute-start.10 = (bf16[80,8192]{1,0:T(8,128)(2,1)}, bf16[80,8192]{1,0:T(8,128)(2,1)}, u32[]{:S(2)}, u32[]{:S(2)}) collective-permute-start(bf16[80,8192]{1,0:T(8,128)(2,1)} %get-tuple-element.57), channel_id=1, source_target_pairs={{0,4},{4,8},{8,12},{12,0},{1,5},{5,9},{9,13},{13,1},{2,6},{6,10},{... | collective-permute-start | bytes 3932168 | tf_op jit(solution)/shard_map/ppermute | solution.py:507
  88.5 41.6 %collective-permute-start.11 = (bf16[64,8192]{1,0:T(8,128)(2,1)}, bf16[64,8192]{1,0:T(8,128)(2,1)}, u32[]{:S(2)}, u32[]{:S(2)}) collective-permute-start(bf16[64,8192]{1,0:T(8,128)(2,1)} %get-tuple-element.58), channel_id=1, source_target_pairs={{0,12},{4,0},{8,4},{12,8},{1,13},{5,1},{9,5},{13,9},{2,14},{6,2},{... | collective-permute-start | bytes 3145736 | tf_op jit(solution)/shard_map/ppermute | solution.py:507
  117.0 13.2 %collective-permute-start.13 = (bf16[32,8192]{1,0:T(8,128)(2,1)}, bf16[32,8192]{1,0:T(8,128)(2,1)}, u32[]{:S(2)}, u32[]{:S(2)}) collective-permute-start(bf16[32,8192]{1,0:T(8,128)(2,1)} %slice.105), channel_id=1, source_target_pairs={{0,12},{4,0},{8,4},{12,8},{1,13},{5,1},{9,5},{13,9},{2,14},{6,2},{... | collective-permute-start | bytes 1572872 | tf_op jit(solution)/shard_map/ppermute | solution.py:515
  117.9 12.2 %collective-permute-start.12 = (bf16[16,8192]{1,0:T(8,128)(2,1)S(1)}, bf16[16,8192]{1,0:T(8,128)(2,1)S(1)}, u32[]{:S(2)}, u32[]{:S(2)}) collective-permute-start(bf16[16,8192]{1,0:T(8,128)(2,1)S(1)} %slice.104), channel_id=1, source_target_pairs={{0,4},{4,8},{8,12},{12,0},{1,5},{5,9},{9,13},{13,1},{2,6},{6,10},{... | collective-permute-start | bytes 786440 | tf_op jit(solution)/shard_map/ppermute | solution.py:514
  144.6 30.3 %collective-permute-start.17 = (bf16[576,1024]{1,0:T(8,128)(2,1)}, bf16[576,1024]{1,0:T(8,128)(2,1)}, u32[]{:S(2)}, u32[]{:S(2)}) collective-permute-start(bf16[576,1024]{1,0:T(8,128)(2,1)} %bitcast.21), channel_id=1, source_target_pairs={{0,1},{1,2},{2,3},{3,0},{4,5},{5,6},{6,7},{7,4},{8,9},{9,10},{10,1... | collective-permute-start | bytes 3538952 | tf_op jit(solution)/shard_map/ppermute | solution.py:461
  149.7 17.0 %collective-permute-start.15 = (bf16[96,4224]{1,0:T(8,128)(2,1)}, bf16[96,4224]{1,0:T(8,128)(2,1)S(1)}, u32[]{:S(2)}, u32[]{:S(2)}) collective-permute-start(bf16[96,4224]{1,0:T(8,128)(2,1)} %get-tuple-element.75), channel_id=1, source_target_pairs={{0,12},{4,0},{8,4},{12,8},{1,13},{5,1},{9,5},{13,9},{2,14},{6,2},{... | collective-permute-start | bytes 2433032 | tf_op jit(solution)/shard_map/ppermute | solution.py:461
  150.5 17.4 %collective-permute-start.14 = (bf16[96,4224]{1,0:T(8,128)(2,1)}, bf16[96,4224]{1,0:T(8,128)(2,1)S(1)}, u32[]{:S(2)}, u32[]{:S(2)}) collective-permute-start(bf16[96,4224]{1,0:T(8,128)(2,1)} %get-tuple-element.74.refs_12_), channel_id=1, source_target_pairs={{0,4},{4,8},{8,12},{12,0},{1,5},{5,9},{9,13},{13,1},{2,6},{6,10},{... | collective-permute-start | bytes 2433032 | tf_op jit(solution)/shard_map/ppermute | solution.py:461
  151.7 26.4 %collective-permute-start.18 = (bf16[576,1024]{1,0:T(8,128)(2,1)}, bf16[576,1024]{1,0:T(8,128)(2,1)S(1)}, u32[]{:S(2)}, u32[]{:S(2)}) collective-permute-start(bf16[576,1024]{1,0:T(8,128)(2,1)} %bitcast.22), channel_id=1, source_target_pairs={{0,3},{1,0},{2,1},{3,2},{4,7},{5,4},{6,5},{7,6},{8,11},{9,8},{10,9... | collective-permute-start | bytes 3538952 | tf_op jit(solution)/shard_map/ppermute | solution.py:461
  153.6 14.3 %copy-start.25 = (bf16[48,4224]{1,0:T(8,128)(2,1)S(1)}, bf16[48,4224]{1,0:T(8,128)(2,1)}, u32[]{:S(2)}) copy-start(bf16[48,4224]{1,0:T(8,128)(2,1)} %copy-done.24) | copy-start | bytes 1216516
  169.4 14.8 %collective-permute-start.21 = (bf16[48,4224]{1,0:T(8,128)(2,1)S(1)}, bf16[48,4224]{1,0:T(8,128)(2,1)S(1)}, u32[]{:S(2)}, u32[]{:S(2)}) collective-permute-start(bf16[48,4224]{1,0:T(8,128)(2,1)S(1)} %get-tuple-element.85), channel_id=1, source_target_pairs={{0,4},{4,8},{8,12},{12,0},{1,5},{5,9},{9,13},{13,1},{2,6},{6,10},{... | collective-permute-start | bytes 1216520 | tf_op jit(solution)/shard_map/ppermute | solution.py:466
  170.1 15.5 %collective-permute-start.22 = (bf16[48,4224]{1,0:T(8,128)(2,1)}, bf16[48,4224]{1,0:T(8,128)(2,1)}, u32[]{:S(2)}, u32[]{:S(2)}) collective-permute-start(bf16[48,4224]{1,0:T(8,128)(2,1)} %get-tuple-element.81.refs_0_), channel_id=1, source_target_pairs={{0,12},{4,0},{8,4},{12,8},{1,13},{5,1},{9,5},{13,9},{2,14},{6,2},{... | collective-permute-start | bytes 1216520 | tf_op jit(solution)/shard_map/ppermute | solution.py:466
  174.9 29.2 %collective-permute-start.16 = (bf16[144,4224]{1,0:T(8,128)(2,1)}, bf16[144,4224]{1,0:T(8,128)(2,1)}, u32[]{:S(2)}, u32[]{:S(2)}) collective-permute-start(bf16[144,4224]{1,0:T(8,128)(2,1)} %get-tuple-element.77), channel_id=1, source_target_pairs={{0,4},{4,8},{8,12},{12,0},{1,5},{5,9},{9,13},{13,1},{2,6},{6,10},{... | collective-permute-start | bytes 3649544 | tf_op jit(solution)/shard_map/ppermute | solution.py:466
  174.9 29.2 %collective-permute-start.19 = (bf16[144,4224]{1,0:T(8,128)(2,1)}, bf16[144,4224]{1,0:T(8,128)(2,1)}, u32[]{:S(2)}, u32[]{:S(2)}) collective-permute-start(bf16[144,4224]{1,0:T(8,128)(2,1)} %get-tuple-element.82.refs_1_), channel_id=1, source_target_pairs={{0,12},{4,0},{8,4},{12,8},{1,13},{5,1},{9,5},{13,9},{2,14},{6,2},{... | collective-permute-start | bytes 3649544 | tf_op jit(solution)/shard_map/ppermute | solution.py:466
  182.5 47.6 %collective-permute-start.27 = (bf16[1152,1024]{1,0:T(8,128)(2,1)}, bf16[1152,1024]{1,0:T(8,128)(2,1)}, u32[]{:S(2)}, u32[]{:S(2)}) collective-permute-start(bf16[1152,1024]{1,0:T(8,128)(2,1)} %get-tuple-element.87), channel_id=1, source_target_pairs={{0,3},{1,0},{2,1},{3,2},{4,7},{5,4},{6,5},{7,6},{8,11},{9,8},{10,9... | collective-permute-start | bytes 7077896 | tf_op jit(solution)/shard_map/ppermute | solution.py:466
  185.0 48.6 %collective-permute-start.26 = (bf16[1152,1024]{1,0:T(8,128)(2,1)S(1)}, bf16[1152,1024]{1,0:T(8,128)(2,1)}, u32[]{:S(2)}, u32[]{:S(2)}) collective-permute-start(bf16[1152,1024]{1,0:T(8,128)(2,1)S(1)} %get-tuple-element.83.refs_1_), channel_id=1, source_target_pairs={{0,1},{1,2},{2,3},{3,0},{4,5},{5,6},{6,7},{7,4},{8,9},{9,10},{10,1... | collective-permute-start | bytes 7077896 | tf_op jit(solution)/shard_map/ppermute | solution.py:466
  187.3 27.3 %collective-permute-start.23 = (bf16[48,4224]{1,0:T(8,128)(2,1)S(1)}, bf16[48,4224]{1,0:T(8,128)(2,1)S(1)}, u32[]{:S(2)}, u32[]{:S(2)}) collective-permute-start(bf16[48,4224]{1,0:T(8,128)(2,1)S(1)} %add_convert_fusion.1), channel_id=1, source_target_pairs={{0,64},{16,80},{32,96},{48,112},{64,0},{80,16},{96,32},{112,48},{1... | collective-permute-start | bytes 1216520 | tf_op jit(solution)/shard_map/ppermute | solution.py:554
  206.6 8.0 %collective-permute-start.20 = (bf16[48,4224]{1,0:T(8,128)(2,1)S(1)}, bf16[48,4224]{1,0:T(8,128)(2,1)S(1)}, u32[]{:S(2)}, u32[]{:S(2)}) collective-permute-start(bf16[48,4224]{1,0:T(8,128)(2,1)S(1)} %get-tuple-element.102), channel_id=1, source_target_pairs={{0,96},{16,112},{32,0},{48,16},{64,32},{80,48},{96,64},{112,80},{1... | collective-permute-start | bytes 1216520 | tf_op jit(solution)/shard_map/ppermute | solution.py:554
  207.1 9.2 %collective-permute-start.24 = (bf16[48,4224]{1,0:T(8,128)(2,1)S(1)}, bf16[48,4224]{1,0:T(8,128)(2,1)S(1)}, u32[]{:S(2)}, u32[]{:S(2)}) collective-permute-start(bf16[48,4224]{1,0:T(8,128)(2,1)S(1)} %get-tuple-element.101), channel_id=1, source_target_pairs={{0,32},{16,48},{32,64},{48,80},{64,96},{80,112},{96,0},{112,16},{1... | collective-permute-start | bytes 1216520 | tf_op jit(solution)/shard_map/ppermute | solution.py:554
  216.5 2.4 %collective-permute-start.25 = (bf16[96,4224]{1,0:T(8,128)(2,1)S(1)}, bf16[96,4224]{1,0:T(8,128)(2,1)S(1)}, u32[]{:S(2)}, u32[]{:S(2)}) collective-permute-start(bf16[96,4224]{1,0:T(8,128)(2,1)S(1)} %pad_maximum_fusion), channel_id=1, source_target_pairs={{0,16},{16,0},{32,48},{48,32},{64,80},{80,64},{96,112},{112,96},{1... | collective-permute-start | bytes 2433032 | tf_op jit(solution)/shard_map/ppermute | solution.py:557
  223.3 15.4 %copy-start.11 = (bf16[256,4096]{1,0:T(8,128)(2,1)}, bf16[256,4096]{1,0:T(8,128)(2,1)S(1)}, u32[]{:S(2)}) copy-start(bf16[256,4096]{1,0:T(8,128)(2,1)S(1)} %convolution_convert_fusion.refs_0_) | copy-start | bytes 6291460
  (39 other events, 179.5 us)
